TPU v7x, 32 devices: a whole 2x2x4 slice. The times are simulated.
32 devices in a mesh: tile: 8 (over y, x, core), lev: 4 (over z).
Axes of the slice: x: 2, y: 2, z: 4, core: 2. Of those that a mesh axis runs over, the one named last changes fastest.
Arguments:
- tracer: float32 [2, 72, 16, 512], P(None, 'lev', 'tile'), may hold values from -6 to 6
- u_courant: float32 [72, 16, 512], P('lev', 'tile'), may hold values from -0.45 to 0.45
- v_courant: float32 [72, 16, 512], P('lev', 'tile'), may hold values from -0.45 to 0.45
- surface_flux: float32 [2, 16, 512], P(None, 'tile'), may hold values from -6 to 6
- mixing: float32 [72, 72], replicated, may hold values from 0 to 1
- kernel: float32 [72, 32768], P('lev', 'tile'), may hold values from 0.1 to 1
- column: int32 [32768], P('tile'), may hold values from 0 to 1023
- owner_tile: int32 [32768], P('tile'), may hold values from 0 to 7, as said below
- offset: int32 [32768], P('tile'), may hold values from 0 to 23
- counts: int32 [8], P('tile'), may hold values from 2048 to 4096, as said below
Outputs:
- transported: float32 [2, 72, 16, 512], P(None, 'lev', 'tile')
- evolved: float32 [2, 32768], P(None, 'tile')
Inputs may be any that keep to these rules, and one draw needn't show every extreme that they name: `owner_tile`: among the rows of one device, no owner tile is named by more than 1536 rows; one owner tile, the same for every device, is named by exactly 1536 rows of each device. Rows at position counts[t] and beyond in tile t's block of soundings are unused.
All inputs are finite; a program needn't handle non-finite values.
Results may differ from a plain program's by a relative error of at most 0.0003.
Values sent between devices are 32-bit elements; how exact they have to be, the bound alone decides.
A program may use at most 64 MiB of HBM per device.

v0:
```python
import jax
import jax.numpy as jnp
from jax import lax
from jax.sharding import PartitionSpec as P

NSUB = 2


def from_behind(block, axis, distance):
    devices = range(lax.axis_size(axis))
    route = [((i - distance) % len(devices), i) for i in devices]
    return lax.ppermute(block, axis, route)


def padded(shard, sides, width):
    for axis, dim in sides:
        size, length = (lax.axis_size(axis), shard.shape[dim])
        up = [(i, (i + 1) % size) for i in range(size)]
        down = [(j, i) for i, j in up]
        last = lax.slice_in_dim(shard, length - width, length, axis=dim)
        initial = lax.slice_in_dim(shard, 0, width, axis=dim)
        before = lax.ppermute(last, axis, up)
        after = lax.ppermute(initial, axis, down)
        shard = jnp.concatenate([before, shard, after], axis=dim)
    return shard


def substep(extended, wind_u, wind_v):
    centre = extended[:, :, 1:-1]
    west_cells = extended[:, :, :-2]
    east_cells = extended[:, :, 2:]
    wind_west = wind_u[:, 1:-1]
    wind_east = wind_u[:, 2:]
    wind_lat = wind_v[:, 1:-1]
    flux_west = wind_west * jnp.where(wind_west > 0, west_cells, centre)
    flux_east = wind_east * jnp.where(wind_east > 0, centre, east_cells)
    south_cells = jnp.concatenate([jnp.zeros_like(centre[..., :1]), centre[..., :-1]], axis=-1)
    lat_ids = lax.broadcasted_iota(jnp.int32, wind_lat.shape, 2)
    open_face = jnp.where(lat_ids > 0, wind_lat, jnp.zeros_like(wind_lat))
    flux_south = open_face * jnp.where(wind_lat > 0, south_cells, centre)
    flux_north = jnp.concatenate(
        [flux_south[..., 1:], jnp.zeros_like(flux_south[..., :1])], axis=-1
    )
    return centre - (flux_east - flux_west) - (flux_north - flux_south)


def body(
    tracer, u_courant, v_courant, surface_flux, mixing, kernel, column, owner_tile, offset, counts
):
    scen_count, level_here, lon_here, lat_count = tracer.shape
    lev_id = lax.axis_index("lev")
    on_ground = (lev_id == 0).astype(jnp.float32)
    advected = tracer.at[:, 0].add(on_ground * surface_flux)
    east_column = from_behind(u_courant[:, :1], "tile", -1)
    wind_u_ext = jnp.concatenate([u_courant[:, :1], u_courant, east_column], axis=1)
    wind_v_ext = jnp.concatenate([v_courant[:, :1], v_courant, v_courant[:, :1]], axis=1)
    for sub_step in range(NSUB):
        extended = padded(advected, (("tile", 2),), 1)
        advected = substep(extended, wind_u_ext, wind_v_ext)
    my_rows = lax.dynamic_slice_in_dim(mixing, lev_id * level_here, level_here, 0)
    transported = jnp.einsum(
        "kl,slxy->skxy",
        my_rows,
        lax.all_gather(advected, "lev", axis=1, tiled=True),
        precision=lax.Precision.HIGHEST,
    )
    snd_here = column.shape[0]
    tile_count = lax.axis_size("tile")
    slot_cap = 3 * snd_here // tile_count
    buffer_len = tile_count * slot_cap
    positions = jnp.arange(snd_here, dtype=jnp.int32)
    in_use = positions < counts[0]
    onehot = (owner_tile[:, None] == jnp.arange(tile_count, dtype=jnp.int32)[None, :]).astype(
        jnp.int32
    )
    rank_ids = jnp.sum(jnp.cumsum(onehot, axis=0) * onehot, axis=1) - 1
    slot_ids = jnp.where(in_use, owner_tile * slot_cap + rank_ids, buffer_len)
    level_ids = lev_id * level_here + jnp.arange(level_here, dtype=jnp.int32)
    weighted = jnp.where(level_ids[:, None] >= offset[None, :], kernel, jnp.zeros_like(kernel))
    denominator = jnp.sum(weighted, axis=0)
    source_ids = (
        jnp.full((buffer_len,), snd_here, jnp.int32).at[slot_ids].set(positions, mode="drop")
    )
    filled = source_ids < snd_here
    safe_ids = jnp.minimum(source_ids, snd_here - 1)
    weight_rows = jnp.take(weighted.T, safe_ids, axis=0)
    send_weights = jnp.where(filled[:, None], weight_rows, jnp.zeros_like(weight_rows))
    column_rows = jnp.take(column, safe_ids, axis=0).astype(jnp.float32)
    send_columns = jnp.where(filled, column_rows, jnp.zeros_like(column_rows))[:, None]
    got_weights, got_columns = (
        lax.all_to_all(send_weights, "tile", split_axis=0, concat_axis=0, tiled=True),
        lax.all_to_all(send_columns, "tile", split_axis=0, concat_axis=0, tiled=True),
    )
    column_ids = got_columns[:, 0].astype(jnp.int32)
    field_rows = transported.reshape(scen_count * level_here, lon_here * lat_count).T
    picked = jnp.take(field_rows, column_ids, axis=0).reshape(buffer_len, scen_count, level_here)
    partial_sums = jnp.sum(picked * got_weights[:, None, :], axis=2)
    returned_sums = lax.all_to_all(partial_sums, "tile", split_axis=0, concat_axis=0, tiled=True)
    own_sums = jnp.take(returned_sums, jnp.minimum(slot_ids, buffer_len - 1), axis=0).T
    numerator, total_weight = lax.psum((own_sums, denominator), "lev")
    evolved = jnp.where(
        in_use[None, :], numerator / total_weight[None, :], jnp.zeros_like(numerator)
    )
    return (transported, evolved)


def solution(mesh):
    in_specs = (
        P(None, "lev", "tile", None),
        P("lev", "tile", None),
        P("lev", "tile", None),
        P(None, "tile", None),
        P(),
        P("lev", "tile"),
        P("tile"),
        P("tile"),
        P("tile"),
        P("tile"),
    )
    out_specs = (P(None, "lev", "tile", None), P(None, "tile"))
    return jax.shard_map(body, mesh=mesh, in_specs=in_specs, out_specs=out_specs, check_vma=False)
```

profile of v0, /device:TPU:0, one launch (start us, length us, event | category | flops | bytes accessed | tf_op | source)
XLA Modules:
  0.0 362.7 jit_solution(2247811336241993717)
XLA Ops:
  1.6 3.4 collective-permute-start
  6.4 2.3 reduce-window.6
  10.9 15.5 %scatter_custom_fusion = s32[12288]{0:T(1024)S(1)} fusion(s32[4096]{0:T(1024)S(1)} %get-tuple-element.39, s32[4096]{0:T(1024)S(1)} %iota.31, s32[]{:T(128)} %constant.110.clone.1), kind=kCustom, calls=%fused_computation.59 | custom fusion | bytes 49156 | tf_op jit(solution)/shard_map/scatter | solution.py:82
  26.5 68.0 %gather_fusion = s32[12288]{0:T(1024)S(1)} fusion(s32[4096]{0:T(1024)S(1)} %copy-done.1, s32[12288]{0:T(1024)S(1)} %fusion.20), kind=kCustom, calls=%fused_computation | custom fusion | bytes 147456 | tf_op jit(solution)/shard_map/jit(_take)/gather | solution.py:88
  95.2 3.3 all-to-all-start
  98.8 2.6 collective-permute-start.1
  101.7 2.0 copy.58
  103.7 2.5 fusion
  106.2 41.1 %gather_fusion.2 = f32[12288,18]{1,0:T(8,128)} fusion(f32[4096,18]{1,0:T(8,128)S(1)} %get-tuple-element.32, s32[12288]{0:T(1024)S(1)} %fusion.20), kind=kCustom, calls=%fused_computation.2 | custom fusion | bytes 1818624 | tf_op jit(solution)/shard_map/jit(_take)/gather | solution.py:86
  147.3 4.4 %copy.59 = f32[8,1536,18]{1,2,0:T(8,128)S(1)} copy(f32[8,1536,18]{2,1,0:T(8,128)} %bitcast.58) | data formatting | bytes 1769472 | tf_op jit(solution)/shard_map/jit(_take)/gather | solution.py:86
  153.6 4.3 %all-to-all-start.1 = ((f32[8,1536,18]{1,2,0:T(8,128)}), f32[8,1536,18]{1,2,0:T(8,128)}, u32[]{:S(2)}, u32[]{:S(2)}) async-start(f32[8,1536,18]{1,2,0:T(8,128)} %select_select_fusion), calls=%async_computation.1 | async-start | bytes 2359296 | tf_op jit(solution)/shard_map/all_to_all | solution.py:91
  158.7 2.6 collective-permute-start.3
  161.8 11.4 %collective-permute-done.3 = f32[2,18,1,512]{3,2,0,1:T(1,128)S(1)} collective-permute-done((f32[2,18,1,512]{3,2,0,1:T(1,128)S(1)}, f32[2,18,1,512]{3,2,0,1:T(1,128)S(1)}, u32[]{:S(2)}, u32[]{:S(2)}) %collective-permute-start.3) | collective-permute-done | bytes 73760 | tf_op jit(solution)/shard_map/ppermute | solution.py:23
  173.2 2.5 collective-permute-done.4
  176.2 16.7 %all_gather.3 = f32[2,72,2,512]{3,2,0,1:T(2,128)S(1)} all-gather(f32[2,18,2,512]{3,2,0,1:T(2,128)S(1)} %fusion.7), channel_id=1, replica_groups=mesh['tile'=8,'lev'=4] {'lev'}, dimensions={1}, use_global_device_ids=true | all-gather | bytes 737280 | tf_op jit(solution)/shard_map/all_gather | solution.py:64
  194.0 41.1 %gather_fusion.1 = f32[12288,36]{1,0:T(8,128)} fusion(f32[1024,36]{1,0:T(8,128)S(1)} %bitcast.56, s32[12288]{0:T(1024)S(1)} %broadcast_clamp_fusion), kind=kCustom, calls=%fused_computation.1 | custom fusion | bytes 3588096 | tf_op jit(solution)/shard_map/jit(_take)/gather | solution.py:96
  235.1 5.7 %copy.57 = f32[12288,36]{0,1:T(8,128)} copy(f32[12288,36]{1,0:T(8,128)} %gather_fusion.1) | data formatting | bytes 3538944 | tf_op jit(solution)/shard_map/jit(_take)/gather | solution.py:96
  246.4 3.5 all-to-all-start.2
  249.9 4.9 %all-to-all-done.2 = f32[8,1536,2]{1,2,0:T(2,128)S(1)} async-done(((f32[8,1536,2]{1,2,0:T(2,128)}), f32[8,1536,2]{1,2,0:T(2,128)S(1)}, u32[]{:S(2)}, u32[]{:S(2)}) %all-to-all-start.2) | async-done | bytes 98336 | tf_op jit(solution)/shard_map/all_to_all | solution.py:98
  254.8 4.0 %copy.62 = f32[8,1536,2]{2,1,0:T(8,128)} copy(f32[8,1536,2]{1,2,0:T(2,128)S(1)} %all-to-all-done.2) | data formatting | bytes 196608 | tf_op jit(solution)/shard_map/all_to_all | solution.py:98
  258.8 16.9 %gather_fusion.3 = f32[4096,2]{1,0:T(8,128)} fusion(f32[12288,2]{1,0:T(8,128)} %bitcast.57, s32[4096]{0:T(1024)S(1)} %get-tuple-element.38), kind=kCustom, calls=%fused_computation.3 | custom fusion | bytes 81920 | tf_op jit(solution)/shard_map/jit(_take)/gather | solution.py:99
  275.7 3.6 select_bitcast_fusion
  279.3 79.0 %all-reduce.4 = (f32[2,4096]{0,1:T(8,128)}, f32[4096]{0:T(1024)S(1)}) all-reduce(f32[2,4096]{0,1:T(8,128)S(1)} %select_bitcast_fusion, f32[4096]{0:T(1024)S(1)} %get-tuple-element.31), channel_id=1, replica_groups=mesh['tile'=8,'lev'=4] {'lev'}, use_global_device_ids=true, to_apply=%region_5.6 | all-reduce | flops 12288 | bytes 98304 | tf_op jit(solution)/shard_map/psum | solution.py:100
  358.3 3.2 divide_select_fusion
  (70 shorter events, 16.2 us)
Async XLA Ops:
  0.6 192.3 %copy-start = (f32[72,72]{1,0:T(8,128)S(1)}, f32[72,72]{1,0:T(8,128)}, u32[]{:S(2)}) copy-start(f32[72,72]{1,0:T(8,128)} %param.16) | copy-start | bytes 62212
  0.6 25.8 %copy-start.1 = (s32[4096]{0:T(1024)S(1)}, s32[4096]{0:T(1024)}, u32[]{:S(2)}) copy-start(s32[4096]{0:T(1024)} %param.18) | copy-start | bytes 49156
  1.6 151.8 %collective-permute-start = (f32[18,1,512]{2,1,0:T(1,128)S(1)}, f32[18,1,512]{2,1,0:T(1,128)S(1)}, u32[]{:S(2)}, u32[]{:S(2)}) collective-permute-start(f32[18,1,512]{2,1,0:T(1,128)S(1)} %slice.83), channel_id=1, source_target_pairs={{4,0},{8,4},{12,8},{16,12},{20,16},{24,20},{28,24},{0,28},{5,1},{9... | collective-permute-start | bytes 110600 | tf_op jit(solution)/shard_map/ppermute | solution.py:12
  26.5 72.1 %copy-start.6 = (f32[2,18,2,512]{3,2,1,0:T(2,128)S(1)}, f32[2,18,2,512]{3,2,1,0:T(2,128)}, u32[]{:S(2)}) copy-start(f32[2,18,2,512]{3,2,1,0:T(2,128)} %param.12) | copy-start | bytes 442372
  26.5 72.1 %copy-start.8 = (f32[2,2,512]{2,1,0:T(2,128)S(1)}, f32[2,2,512]{2,1,0:T(2,128)}, u32[]{:S(2)}) copy-start(f32[2,2,512]{2,1,0:T(2,128)} %param.15) | copy-start | bytes 24580
  26.5 74.9 %copy-start.5 = (f32[18,2,512]{2,1,0:T(2,128)S(1)}, f32[18,2,512]{2,1,0:T(2,128)}, u32[]{:S(2)}) copy-start(f32[18,2,512]{2,1,0:T(2,128)} %param.14) | copy-start | bytes 221188
  26.5 75.2 %copy-start.4 = (f32[18,4096]{1,0:T(8,128)S(1)}, f32[18,4096]{1,0:T(8,128)}, u32[]{:S(2)}) copy-start(f32[18,4096]{1,0:T(8,128)} %param.17) | copy-start | bytes 884740
  94.6 9.1 %copy-start.7 = (s32[4096]{0:T(1024)S(1)}, s32[4096]{0:T(1024)}, u32[]{:S(2)}) copy-start(s32[4096]{0:T(1024)} %param.20) | copy-start | bytes 49156
  95.2 58.4 %all-to-all-start = ((f32[8,1536,1]{1,2,0:T(1,128)}), f32[8,1536,1]{1,2,0:T(1,128)S(1)}, u32[]{:S(2)}, u32[]{:S(2)}) async-start(f32[8,1536,1]{1,2,0:T(1,128)} %bitcast.7), calls=%async_computation | async-start | bytes 98304 | tf_op jit(solution)/shard_map/all_to_all | solution.py:92
  98.8 59.3 %collective-permute-start.1 = (f32[2,18,1,512]{3,2,0,1:T(1,128)S(1)}, f32[2,18,1,512]{3,2,0,1:T(1,128)S(1)}, u32[]{:S(2)}, u32[]{:S(2)}) collective-permute-start(f32[2,18,1,512]{3,2,0,1:T(1,128)S(1)} %get-tuple-element.35), channel_id=1, source_target_pairs={{4,0},{8,4},{12,8},{16,12},{20,16},{24,20},{28,24},{0,28},{5,1},{9... | collective-permute-start | bytes 221192 | tf_op jit(solution)/shard_map/ppermute | solution.py:23
  101.4 56.7 %collective-permute-start.2 = (f32[2,18,1,512]{3,2,0,1:T(1,128)S(1)}, f32[2,18,1,512]{3,2,0,1:T(1,128)S(1)}, u32[]{:S(2)}, u32[]{:S(2)}) collective-permute-start(f32[2,18,1,512]{3,2,0,1:T(1,128)S(1)} %get-tuple-element.36), channel_id=1, source_target_pairs={{0,4},{4,8},{8,12},{12,16},{16,20},{20,24},{24,28},{28,0},{1,5},{5... | collective-permute-start | bytes 221192 | tf_op jit(solution)/shard_map/ppermute | solution.py:22
  151.7 1.7 copy-start.2
  153.6 89.0 %all-to-all-start.1 = ((f32[8,1536,18]{1,2,0:T(8,128)}), f32[8,1536,18]{1,2,0:T(8,128)}, u32[]{:S(2)}, u32[]{:S(2)}) async-start(f32[8,1536,18]{1,2,0:T(8,128)} %select_select_fusion), calls=%async_computation.1 | async-start | bytes 2359296 | tf_op jit(solution)/shard_map/all_to_all | solution.py:91
  158.7 14.5 %collective-permute-start.3 = (f32[2,18,1,512]{3,2,0,1:T(1,128)S(1)}, f32[2,18,1,512]{3,2,0,1:T(1,128)S(1)}, u32[]{:S(2)}, u32[]{:S(2)}) collective-permute-start(f32[2,18,1,512]{3,2,0,1:T(1,128)S(1)} %get-tuple-element.33), channel_id=1, source_target_pairs={{4,0},{8,4},{12,8},{16,12},{20,16},{24,20},{28,24},{0,28},{5,1},{9... | collective-permute-start | bytes 221192 | tf_op jit(solution)/shard_map/ppermute | solution.py:23
  161.3 14.4 %collective-permute-start.4 = (f32[2,18,1,512]{3,2,0,1:T(1,128)S(1)}, f32[2,18,1,512]{3,2,0,1:T(1,128)S(1)}, u32[]{:S(2)}, u32[]{:S(2)}) collective-permute-start(f32[2,18,1,512]{3,2,0,1:T(1,128)S(1)} %get-tuple-element.34), channel_id=1, source_target_pairs={{0,4},{4,8},{8,12},{12,16},{16,20},{20,24},{24,28},{28,0},{1,5},{5... | collective-permute-start | bytes 221192 | tf_op jit(solution)/shard_map/ppermute | solution.py:22
  193.6 41.4 %copy-start.3 = (f32[2,18,2,512]{3,2,1,0:T(2,128)}, f32[2,18,2,512]{3,2,1,0:T(2,128)S(1)}, u32[]{:S(2)}) copy-start(f32[2,18,2,512]{3,2,1,0:T(2,128)S(1)} %copy.63) | copy-start | bytes 442372
  246.4 8.5 %all-to-all-start.2 = ((f32[8,1536,2]{1,2,0:T(2,128)}), f32[8,1536,2]{1,2,0:T(2,128)S(1)}, u32[]{:S(2)}, u32[]{:S(2)}) async-start(f32[8,1536,2]{1,2,0:T(2,128)} %bitcast.14), calls=%async_computation.2 | async-start | bytes 196608 | tf_op jit(solution)/shard_map/all_to_all | solution.py:98
where the time goes:
time: 364 us; the launch traced here: 363 us
  local copies, waits for them, and re-layouts  207 us (57%)
  blocking collectives  95.6 us (26%)
  starting transfers between devices  19.8 us (5%)
  other arithmetic  19.1 us (5%)
  waiting for transfers between devices  18.9 us (5%)
    psum x1, blocking collectives, body(): numerator, total_weight = lax.psum((own_sums, denominator), 'lev')  79 us
    gather x1, local copies, waits for them, and re-layouts, body(): column_rows = jnp.take(column, safe_ids, axis=0).astype(jnp.float32)  68 us
    gather x3, local copies, waits for them, and re-layouts, body(): jnp.take(field_rows, column_ids, axis=0)  48.6 us
    gather x2, local copies, waits for them, and re-layouts, body(): weight_rows = jnp.take(weighted.T, safe_ids, axis=0)  45.5 us
    gather x1, local copies, waits for them, and re-layouts, body(): jnp.take(returned_sums, jnp.minimum(slot_ids, buffer_len - 1), axis=0)  16.9 us
    all_gather x1, blocking collectives, body(): lax.all_gather(advected, 'lev', axis=1, tiled=True)  16.7 us
    scatter x1, local copies, waits for them, and re-layouts, body(): jnp.full((buffer_len,), snd_here, jnp.int32).at[slot_ids]  15.5 us
    ppermute x2, waiting for transfers between devices, padded(): after = lax.ppermute(initial, axis, down)  11.4 us
  transfers between devices with their start and end apart: 8, of which 3 were waited for; matrix products, arithmetic and copies ran while one was open for 53% of the time, Pallas kernels for 0%

commit v1 on v0

v1 whole, which is shorter than its diff:
```python
import functools
import jax
import jax.numpy as jnp
from jax import lax
from jax.experimental import pallas as pl
from jax.experimental.pallas import tpu as pltpu
from jax.sharding import PartitionSpec as P

NSUB = 2
PAD = 24
KPAD = 32
NB = 256
GROUP = 8
MESH = pl.DeviceIdType.MESH


def split(x):
    high = x.astype(jnp.bfloat16)
    low = (x - high.astype(jnp.float32)).astype(jnp.bfloat16)
    return high, low


def flip(index, bit):
    return index + bit - 2 * bit * ((index // bit) % 2)


def substep(cells, winds, lat_winds, lat_ids):
    count = len(lat_winds)
    size = cells[0].shape[-1]
    west = [
        winds[i] * jnp.where(winds[i] > 0, cells[i], cells[i + 1]) for i in range(count + 1)
    ]
    result = []
    for i in range(count):
        centre = cells[i + 1]
        south_cells = pltpu.roll(centre, 1, 1)
        south = lat_winds[i] * jnp.where(lat_winds[i] > 0, south_cells, centre)
        south = jnp.where(lat_ids > 0, south, 0.0)
        north = pltpu.roll(south, size - 1, 1)
        result.append(centre - (west[i + 1] - west[i]) - (north - south))
    return result


def kernel_body(
    dims,
    tracer, u_ref, v_ref, flux, mix, kern, column, owner, offset, counts,
    out, evolved,
    cur, halo_w, halo_e, halo_u, levs, rhs, gathered, lhs, onehot, lon_of, weight,
    nums, dens, pad,
    h_send, h_recv, u_sem, z_send, z_recv, g_send, g_recv, n_send, n_recv,
):
    scen, lev_here, lon_here, nlat, snd, tiles, nlev = dims
    me, lev = lax.axis_index("tile"), lax.axis_index("lev")
    east, west = lax.rem(me + 1, tiles), lax.rem(me + tiles - 1, tiles)
    bits = [1 << k for k in range(tiles.bit_length() - 1)]
    peers = [lax.rem(lev + r, nlev) for r in range(1, nlev)]

    barrier = pltpu.get_barrier_semaphore()
    friends = [(east, lev), (west, lev)]
    friends += [(flip(me, b), lev) for b in bits]
    friends += [(me, p) for p in peers]
    for friend in friends:
        pl.semaphore_signal(barrier, inc=1, device_id=friend, device_id_type=MESH)

    row_ids = lax.broadcasted_iota(jnp.int32, (lev_here, nlat), 0)
    lat_ids = lax.broadcasted_iota(jnp.int32, (lev_here, nlat), 1)
    bottom = jnp.logical_and(row_ids == 0, lev == 0)
    for s in range(scen):
        for i in range(lon_here):
            here = tracer[s, i]
            cur[0, s, i] = jnp.where(bottom, here + flux[s, pl.ds(i, 1)], here)
    pl.semaphore_wait(barrier, len(friends))

    def remote(src, dst, send, recv, device):
        return pltpu.make_async_remote_copy(
            src_ref=src, dst_ref=dst, send_sem=send, recv_sem=recv,
            device_id=device, device_id_type=MESH,
        )

    pending = []

    def send_halo(step, s):
        to_east = remote(
            cur.at[step, s, lon_here - 1], halo_w.at[step, s],
            h_send.at[step, s, 0], h_recv.at[step, s, 0], (east, lev),
        )
        to_west = remote(
            cur.at[step, s, 0], halo_e.at[step, s],
            h_send.at[step, s, 1], h_recv.at[step, s, 1], (west, lev),
        )
        to_east.start()
        to_west.start()
        pending.extend([to_east, to_west])
        return to_east, to_west

    u_copy = remote(u_ref.at[0], halo_u, u_sem.at[0], u_sem.at[1], (west, lev))
    u_copy.start()
    pending.append(u_copy)
    halos = {(0, s): send_halo(0, s) for s in range(scen)}

    level_ids = lev * lev_here + lax.broadcasted_iota(jnp.int32, (lev_here, NB), 0)
    lat_rows = lax.broadcasted_iota(jnp.int32, (nlat, NB), 0)

    def prepare(nb, carry):
        at = pl.ds(pl.multiple_of(nb * NB, NB), NB)
        col = column[:, at]
        lon_in = col // nlat
        lat = col - lon_in * nlat
        onehot[:, at] = (lat_rows == lat).astype(jnp.float32).astype(jnp.bfloat16)
        lon_of[:, at] = owner[:, at] * lon_here + lon_in
        used_weight = jnp.where(level_ids >= offset[:, at], kern[:, at], 0.0)
        weight[:, at] = used_weight
        dens[lev, :, at] = jnp.sum(used_weight, axis=0, keepdims=True)
        return carry

    lax.fori_loop(0, snd // NB, prepare, 0)
    pad[...] = jnp.zeros_like(pad)

    u_copy.wait_recv()
    for step in range(NSUB):
        for s in range(scen):
            for copy in halos[(step, s)]:
                copy.wait_recv()
            cells = [halo_w[step, s]] + [cur[step, s, i] for i in range(lon_here)]
            cells.append(halo_e[step, s])
            winds = [u_ref[i] for i in range(lon_here)] + [halo_u[...]]
            new = substep(cells, winds, [v_ref[i] for i in range(lon_here)], lat_ids)
            if step < NSUB - 1:
                for i in range(lon_here):
                    cur[step + 1, s, i] = new[i]
                halos[(step + 1, s)] = send_halo(step + 1, s)
            else:
                for i in range(lon_here):
                    levs[s, lev, i] = new[i]
                copies = []
                for r, peer in enumerate(peers):
                    copy = remote(
                        levs.at[s, lev], levs.at[s, lev],
                        z_send.at[s, r], z_recv.at[s, r], (me, peer),
                    )
                    copy.start()
                    copies.append(copy)
                pending.extend(copies)
                halos[("z", s)] = copies

    den_copies = []
    for r, peer in enumerate(peers):
        copy = remote(
            dens.at[lev], dens.at[lev],
            n_send.at[scen, r], n_recv.at[scen, r], (me, peer),
        )
        copy.start()
        den_copies.append(copy)

    routes = {}
    for s in range(scen):
        for copy in halos[("z", s)]:
            copy.wait_recv()
        for i in range(lon_here):
            for z in range(nlev):
                pad[0:lev_here] = levs[s, z, i]
                high, low = split(pad[...])
                rhs[z * KPAD:(z + 1) * KPAD] = high
                rhs[(nlev + z) * KPAD:(nlev + z + 1) * KPAD] = low
            both = jnp.dot(mix[...], rhs[...], preferred_element_type=jnp.float32)
            total = both[0:PAD] + both[PAD:2 * PAD]
            gathered[s, 0, i] = total[0:lev_here]
            out[s, i] = total[0:lev_here]
        order = bits[::-1] if s % 2 == 0 else bits[-2::-1][:-1] + [bits[-1]] + bits[:1]
        held, sent = [0], []
        routes[s] = []
        for bit in order:
            step_copies = []
            for m in held:
                copy = remote(
                    gathered.at[s, m], gathered.at[s, m + bit],
                    g_send.at[s, m + bit], g_recv.at[s, m + bit], (flip(me, bit), lev),
                )
                step_copies.append((m, copy))
            routes[s].append(step_copies)
            held = held + [m + bit for m in held]
    for s in range(scen):
        for _, copy in routes[s][0]:
            copy.start()
    for k in range(1, len(bits)):
        for s in range(scen):
            for _, copy in routes[s][k - 1]:
                copy.wait_recv()
            for _, copy in routes[s][k]:
                copy.start()

    rows = GROUP * lon_here * PAD
    for s in range(scen):
        for _, copy in routes[s][-1]:
            copy.wait_recv()
        for m in range(tiles):
            group, inner = m // GROUP, m % GROUP
            for i in range(lon_here):
                pad[0:lev_here] = gathered[s, m, i]
                value = pad[0:PAD] if i == 0 else jnp.concatenate([value, pad[0:PAD]], axis=0)
            high, low = split(value)
            at = inner * lon_here * PAD
            lhs[group, at:at + lon_here * PAD] = high
            lhs[group, rows + at:rows + at + lon_here * PAD] = low

        def sample(nb, carry):
            at = pl.ds(pl.multiple_of(nb * NB, NB), NB)
            hot = onehot[:, at]
            lon_ids = jnp.broadcast_to(lon_of[:, at], (PAD, NB))

            def one_group(group, acc):
                found = jnp.dot(lhs[group], hot, preferred_element_type=jnp.float32)
                for inner in range(GROUP):
                    tile = jnp.bitwise_xor(me, group * GROUP + inner)
                    for i in range(lon_here):
                        r = (inner * lon_here + i) * PAD
                        block = found[r:r + PAD] + found[rows + r:rows + r + PAD]
                        acc = jnp.where(lon_ids == tile * lon_here + i, block, acc)
                return acc

            acc = jnp.zeros((PAD, NB), jnp.float32)
            if tiles == GROUP:
                acc = one_group(0, acc)
            else:
                acc = lax.fori_loop(0, tiles // GROUP, one_group, acc)
            terms = acc[0:lev_here] * weight[:, at]
            nums[s, lev, :, at] = jnp.sum(terms, axis=0, keepdims=True)
            return carry

        lax.fori_loop(0, snd // NB, sample, 0)
        copies = []
        for r, peer in enumerate(peers):
            copy = remote(
                nums.at[s, lev], nums.at[s, lev],
                n_send.at[s, r], n_recv.at[s, r], (me, peer),
            )
            copy.start()
            copies.append(copy)
        halos[("n", s)] = copies

    for copy in den_copies:
        copy.wait_recv()
    den = dens[0]
    for z in range(1, nlev):
        den = den + dens[z]
    in_use = lax.broadcasted_iota(jnp.int32, (1, snd), 1) < counts[0]
    for s in range(scen):
        for copy in halos[("n", s)]:
            copy.wait_recv()
        num = nums[s, 0]
        for z in range(1, nlev):
            num = num + nums[s, z]
        evolved[s] = jnp.where(in_use, num / den, 0.0)
        pending.extend(halos[("n", s)])
    pending.extend(den_copies)
    for s in range(scen):
        for step_copies in routes[s]:
            pending.extend(copy for _, copy in step_copies)
    for copy in pending:
        copy.wait_send()


def body(
    tracer, u_courant, v_courant, surface_flux, mixing, kernel, column, owner_tile, offset, counts
):
    scen, lev_here, lon_here, nlat = tracer.shape
    snd = column.shape[0]
    tiles, nlev = lax.axis_size("tile"), lax.axis_size("lev")
    lev = lax.axis_index("lev")
    rows = lax.dynamic_slice_in_dim(mixing, lev * lev_here, lev_here, 0)
    rows = rows.reshape(lev_here, nlev, lev_here)
    rows = jnp.pad(rows, ((0, PAD - lev_here), (0, 0), (0, KPAD - lev_here)))
    rows = rows.reshape(PAD, nlev * KPAD)
    high = lax.reduce_precision(rows, 8, 7)
    low = rows - high
    mix = jnp.concatenate(
        [
            jnp.concatenate([high, high], axis=1),
            jnp.concatenate([low, jnp.zeros_like(low)], axis=1),
        ],
        axis=0,
    ).astype(jnp.bfloat16)
    f32, bf16 = jnp.float32, jnp.bfloat16
    block = (lev_here, nlat)
    dma = pltpu.SemaphoreType.DMA
    vmem = pl.BlockSpec(memory_space=pltpu.VMEM)
    groups = tiles // GROUP
    out, evolved = pl.pallas_call(
        functools.partial(kernel_body, (scen, lev_here, lon_here, nlat, snd, tiles, nlev)),
        out_shape=(
            jax.ShapeDtypeStruct((scen, lon_here) + block, f32),
            jax.ShapeDtypeStruct((scen, 1, snd), f32),
        ),
        in_specs=[vmem] * 9 + [pl.BlockSpec(memory_space=pltpu.SMEM)],
        out_specs=(vmem, vmem),
        scratch_shapes=[
            pltpu.VMEM((NSUB, scen, lon_here) + block, f32),
            pltpu.VMEM((NSUB, scen) + block, f32),
            pltpu.VMEM((NSUB, scen) + block, f32),
            pltpu.VMEM(block, f32),
            pltpu.VMEM((scen, nlev, lon_here) + block, f32),
            pltpu.VMEM((2 * nlev * KPAD, nlat), bf16),
            pltpu.VMEM((scen, tiles, lon_here) + block, f32),
            pltpu.VMEM((groups, 2 * GROUP * lon_here * PAD, nlat), bf16),
            pltpu.VMEM((nlat, snd), bf16),
            pltpu.VMEM((1, snd), jnp.int32),
            pltpu.VMEM((lev_here, snd), f32),
            pltpu.VMEM((scen, nlev, 1, snd), f32),
            pltpu.VMEM((nlev, 1, snd), f32),
            pltpu.VMEM((KPAD, nlat), f32),
            dma((NSUB, scen, 2)),
            dma((NSUB, scen, 2)),
            dma((2,)),
            dma((scen, nlev - 1)),
            dma((scen, nlev - 1)),
            dma((scen, tiles)),
            dma((scen, tiles)),
            dma((scen + 1, nlev - 1)),
            dma((scen + 1, nlev - 1)),
        ],
        compiler_params=pltpu.CompilerParams(
            collective_id=0, has_side_effects=True, vmem_limit_bytes=56 * 2**20
        ),
    )(
        tracer.transpose(0, 2, 1, 3),
        u_courant.transpose(1, 0, 2),
        v_courant.transpose(1, 0, 2),
        surface_flux,
        mix,
        kernel,
        column[None],
        owner_tile[None],
        offset[None],
        counts,
    )
    return out.transpose(0, 2, 1, 3), evolved[:, 0]


def solution(mesh):
    in_specs = (
        P(None, "lev", "tile", None),
        P("lev", "tile", None),
        P("lev", "tile", None),
        P(None, "tile", None),
        P(),
        P("lev", "tile"),
        P("tile"),
        P("tile"),
        P("tile"),
        P("tile"),
    )
    out_specs = (P(None, "lev", "tile", None), P(None, "tile"))
    return jax.shard_map(body, mesh=mesh, in_specs=in_specs, out_specs=out_specs, check_vma=False)
```

time: 364 us -> 67.9 us (0.19)
  local copies, waits for them, and re-layouts: 207 us -> 4.29 us
  blocking collectives: 95.6 us -> 0 us
  Pallas kernels: 0 us -> 61 us
  starting transfers between devices: 19.8 us -> 0 us
  waiting for transfers between devices: 18.9 us -> 0 us
  other arithmetic: 19.1 us -> 0.62 us
    gather x7 -> x0, local copies, waits for them, and re-layouts: 179 us -> none  [the longest x1 68 us: body(): column_rows = jnp.take(column, safe_ids, axis=0).astype(jnp.float32)]
    psum x1 -> x0, blocking collectives: 79 us -> none  [body(): numerator, total_weight = lax.psum((own_sums, denominator), 'lev')]
    pallas_call x0 -> x1, Pallas kernels: none -> 61 us  [body(): pl.pallas_call(functools.partial(kernel_body, (scen, lev_here, lon_here,...]
    all_gather x1 -> x0, blocking collectives: 16.7 us -> none  [body(): lax.all_gather(advected, 'lev', axis=1, tiled=True)]
    scatter x1 -> x0, local copies, waits for them, and re-layouts: 15.5 us -> none  [body(): jnp.full((buffer_len,), snd_here, jnp.int32).at[slot_ids]]
    ppermute x5 -> x0, waiting for transfers between devices: 13.9 us -> none  [the longest x2 11.4 us: padded(): after = lax.ppermute(initial, axis, down)]
    all_to_all x3 -> x0, starting transfers between devices: 11.2 us -> none  [the longest x1 4.29 us: body(): lax.all_to_all(send_weights, 'tile', split_axis=0, concat_axis=0, tiled=T...]
    select_n x6 -> x0, other arithmetic: 8.73 us -> none  [the longest x1 3.6 us: body(): jnp.take(returned_sums, jnp.minimum(slot_ids, buffer_len - 1), axis=0)]
  transfers between devices with their start and end apart: 8 -> 0, of which waited for: 3 -> 0; matrix products, arithmetic and copies ran while one was open for 53% -> 0% of each run, Pallas kernels for 0% -> 0%
where the time goes in v1:
time: 67.9 us; the launch traced here: 67.3 us
  Pallas kernels  61 us (90%)
  local copies, waits for them, and re-layouts  4.29 us (6%)
  between operations  1.37 us (2%)
    pallas_call x1, Pallas kernels, body(): pl.pallas_call(functools.partial(kernel_body, (scen, lev_here, lon_here,...  61 us
    unnamed x13, local copies, waits for them, and re-layouts  3.39 us

profile of v1, /device:TPU:0, one launch (start us, length us, event | category | flops | bytes accessed | tf_op | source)
XLA Modules:
  0.0 67.3 jit_solution(4520306904278745180)
XLA Ops:
  0.6 0.0 copy-start
  0.6 0.0 copy-start.1
  1.3 0.1 copy-done
  1.4 0.1 reshape.10
  1.5 0.1 reshape.11
  1.6 0.6 fusion.1.mix
  2.2 0.0 copy-done.1
  2.2 0.0 copy-start.2
  2.2 0.0 copy-start.3
  2.2 0.7 %copy.21 = f32[2,18,2,512]{3,1,2,0:T(8,128)} copy(f32[2,18,2,512]{3,2,1,0:T(2,128)S(1)} %copy-done.1) | data formatting | bytes 294912 | tf_op args[0]
  3.0 0.2 copy-done.2
  3.1 0.1 copy-done.3
  3.2 0.7 %copy_bitcast_fusion.1 = (f32[2,18,512]{2,1,0:T(8,128)}, f32[2,18,512]{2,1,0:T(8,128)}) fusion(f32[18,2,512]{2,1,0:T(2,128)S(1)} %copy-done.2, f32[18,2,512]{2,1,0:T(2,128)S(1)} %copy-done.3), kind=kLoop, calls=%fused_computation.1 | loop fusion | bytes 294912 | tf_op jit(solution)/shard_map/transpose | solution.py:327
  3.9 61.0 %shard_map.113 = (f32[2,2,18,512]{3,2,1,0:T(8,128)}, f32[2,1,4096]{2,1,0:T(1,128)}) custom-call(f32[2,2,18,512]{3,2,1,0:T(8,128)} %bitcast.14, f32[2,18,512]{2,1,0:T(8,128)} %get-tuple-element.11.u_ref, f32[2,18,512]{2,1,0:T(8,128)} %get-tuple-element.10.v_ref, f32[2,2,512]{2,1,0:T(2,128)} %flux.1, bf16[48,256]{1,0:T(8,128)(2,1)} %fusion.1.mix, ...), custom_call_target="tpu_custom_call" | custom-call | tf_op jit(solution)/shard_map/pallas_call | solution.py:288
  64.9 0.0 copy-start.4
  64.9 1.7 %copy.15 = f32[2,18,2,512]{3,2,1,0:T(2,128)} copy(f32[2,18,2,512]{3,1,2,0:T(8,128)} %bitcast.15) | data formatting | bytes 294912
  66.6 0.0 copy-done.4
  66.6 0.6 copy.22
  (3 shorter events, 0.0 us)
Async XLA Ops:
  0.6 0.8 %copy-start = (f32[72,72]{1,0:T(8,128)S(1)}, f32[72,72]{1,0:T(8,128)}, u32[]{:S(2)}) copy-start(f32[72,72]{1,0:T(8,128)} %param.14) | copy-start | bytes 62212
  0.6 1.6 %copy-start.1 = (f32[2,18,2,512]{3,2,1,0:T(2,128)S(1)}, f32[2,18,2,512]{3,2,1,0:T(2,128)}, u32[]{:S(2)}) copy-start(f32[2,18,2,512]{3,2,1,0:T(2,128)} %param.10) | copy-start | bytes 442372
  2.2 0.9 %copy-start.2 = (f32[18,2,512]{2,1,0:T(2,128)S(1)}, f32[18,2,512]{2,1,0:T(2,128)}, u32[]{:S(2)}) copy-start(f32[18,2,512]{2,1,0:T(2,128)} %param.12) | copy-start | bytes 221188
  2.2 1.0 %copy-start.3 = (f32[18,2,512]{2,1,0:T(2,128)S(1)}, f32[18,2,512]{2,1,0:T(2,128)}, u32[]{:S(2)}) copy-start(f32[18,2,512]{2,1,0:T(2,128)} %param.11) | copy-start | bytes 221188
  64.9 1.7 %copy-start.4 = (f32[2,1,4096]{2,1,0:T(1,128)S(1)}, f32[2,1,4096]{2,1,0:T(1,128)}, u32[]{:S(2)}) copy-start(f32[2,1,4096]{2,1,0:T(1,128)} %get-tuple-element.5) | copy-start | bytes 98308

commit v2 on v1

--- a/solution.py
+++ b/solution.py
@@ -45,9 +45,9 @@
     dims,
     tracer, u_ref, v_ref, flux, mix, kern, column, owner, offset, counts,
     out, evolved,
-    cur, halo_w, halo_e, halo_u, levs, rhs, gathered, lhs, onehot, lon_of, weight,
+    cur, halo_w, halo_e, halo_u, levs, mixed, rhs, gathered, lhs, onehot, lon_of, weight,
     nums, dens, pad,
-    h_send, h_recv, u_sem, z_send, z_recv, g_send, g_recv, n_send, n_recv,
+    h_send, h_recv, u_sem, z_send, z_recv, g_send, g_recv, n_send, n_recv, d_send, d_recv,
 ):
     scen, lev_here, lon_here, nlat, snd, tiles, nlev = dims
     me, lev = lax.axis_index("tile"), lax.axis_index("lev")
@@ -100,6 +100,7 @@
 
     level_ids = lev * lev_here + lax.broadcasted_iota(jnp.int32, (lev_here, NB), 0)
     lat_rows = lax.broadcasted_iota(jnp.int32, (nlat, NB), 0)
+    steps = snd // NB
 
     def prepare(nb, carry):
         at = pl.ds(pl.multiple_of(nb * NB, NB), NB)
@@ -113,8 +114,21 @@
         dens[lev, :, at] = jnp.sum(used_weight, axis=0, keepdims=True)
         return carry
 
-    lax.fori_loop(0, snd // NB, prepare, 0)
+    lax.fori_loop(0, steps // 2, prepare, 0)
     pad[...] = jnp.zeros_like(pad)
+
+    half, parity = lev // 2, lev % 2
+    is_end = half == parity
+    mate = half * 2 + 1 - parity
+
+    def z_copy(s, k, src, dst, to):
+        return remote(src, dst, z_send.at[s, k], z_recv.at[s, k], (me, to))
+
+    def raw_copy(s, k, to):
+        return z_copy(s, k, levs.at[s, lev], levs.at[s, lev], to)
+
+    def mixed_copy(s):
+        return z_copy(s, 3, mixed.at[s], gathered.at[s, 0], mate)
 
     u_copy.wait_recv()
     for step in range(NSUB):
@@ -132,67 +146,78 @@
             else:
                 for i in range(lon_here):
                     levs[s, lev, i] = new[i]
-                copies = []
-                for r, peer in enumerate(peers):
-                    copy = remote(
-                        levs.at[s, lev], levs.at[s, lev],
-                        z_send.at[s, r], z_recv.at[s, r], (me, peer),
-                    )
-                    copy.start()
-                    copies.append(copy)
-                pending.extend(copies)
-                halos[("z", s)] = copies
-
+
+                @pl.when(is_end)
+                def _():
+                    raw_copy(s, 2, nlev - 1 - mate).start()
+                    raw_copy(s, 0, mate).start()
+
+                @pl.when(jnp.logical_not(is_end))
+                def _():
+                    raw_copy(s, 1, nlev - 1 - lev).start()
+
+    lax.fori_loop(steps // 2, steps, prepare, 0)
     den_copies = []
     for r, peer in enumerate(peers):
         copy = remote(
             dens.at[lev], dens.at[lev],
-            n_send.at[scen, r], n_recv.at[scen, r], (me, peer),
+            d_send.at[r], d_recv.at[r], (me, peer),
         )
         copy.start()
         den_copies.append(copy)
 
-    routes = {}
-    for s in range(scen):
-        for copy in halos[("z", s)]:
-            copy.wait_recv()
-        for i in range(lon_here):
-            for z in range(nlev):
-                pad[0:lev_here] = levs[s, z, i]
-                high, low = split(pad[...])
-                rhs[z * KPAD:(z + 1) * KPAD] = high
-                rhs[(nlev + z) * KPAD:(nlev + z + 1) * KPAD] = low
-            both = jnp.dot(mix[...], rhs[...], preferred_element_type=jnp.float32)
-            total = both[0:PAD] + both[PAD:2 * PAD]
-            gathered[s, 0, i] = total[0:lev_here]
-            out[s, i] = total[0:lev_here]
-        order = bits[::-1] if s % 2 == 0 else bits[-2::-1][:-1] + [bits[-1]] + bits[:1]
-        held, sent = [0], []
-        routes[s] = []
-        for bit in order:
-            step_copies = []
-            for m in held:
-                copy = remote(
-                    gathered.at[s, m], gathered.at[s, m + bit],
-                    g_send.at[s, m + bit], g_recv.at[s, m + bit], (flip(me, bit), lev),
-                )
-                step_copies.append((m, copy))
-            routes[s].append(step_copies)
+    def mix_levels(s):
+        @pl.when(jnp.logical_not(is_end))
+        def _():
+            raw_copy(s, 0, mate).wait_recv()
+            raw_copy(s, 1, mate).wait_recv()
+            raw_copy(s, 2, mate).wait_recv()
+            for i in range(lon_here):
+                for z in range(nlev):
+                    pad[0:lev_here] = levs[s, z, i]
+                    high, low = split(pad[...])
+                    rhs[z * KPAD:(z + 1) * KPAD] = high
+                    rhs[(nlev + z) * KPAD:(nlev + z + 1) * KPAD] = low
+                both = jnp.dot(mix[...], rhs[...], preferred_element_type=jnp.float32)
+                first = both[0:PAD] + both[PAD:2 * PAD]
+                second = both[2 * PAD:3 * PAD] + both[3 * PAD:4 * PAD]
+                gathered[s, 0, i] = jnp.where(parity == 0, first, second)[0:lev_here]
+                mixed[s, i] = jnp.where(parity == 0, second, first)[0:lev_here]
+            mixed_copy(s).start()
+
+        @pl.when(is_end)
+        def _():
+            mixed_copy(s).wait_recv()
+
+    orders = [bits[::-1], bits[-2:0:-1] + bits[-1:] + bits[:1]]
+
+    def masks_at(s, p):
+        held = [0]
+        for bit in orders[s % 2][:p]:
             held = held + [m + bit for m in held]
-    for s in range(scen):
-        for _, copy in routes[s][0]:
-            copy.start()
-    for k in range(1, len(bits)):
-        for s in range(scen):
-            for _, copy in routes[s][k - 1]:
-                copy.wait_recv()
-            for _, copy in routes[s][k]:
+        return held
+
+    def block_copy(s, m, bit):
+        return remote(
+            gathered.at[s, m], gathered.at[s, m + bit],
+            g_send.at[s, m + bit], g_recv.at[s, m + bit], (flip(me, bit), lev),
+        )
+
+    def forward(s, p):
+        order = orders[s % 2]
+        fresh = [0] if p == 0 else [m + order[p - 1] for m in masks_at(s, p - 1)]
+        for m in fresh:
+            if p > 0:
+                block_copy(s, m - order[p - 1], order[p - 1]).wait_recv()
+            for bit in order[p:]:
+                copy = block_copy(s, m, bit)
                 copy.start()
+                pending.append(copy)
 
     rows = GROUP * lon_here * PAD
-    for s in range(scen):
-        for _, copy in routes[s][-1]:
-            copy.wait_recv()
+    hops = len(bits)
+
+    def load_columns(s):
         for m in range(tiles):
             group, inner = m // GROUP, m % GROUP
             for i in range(lon_here):
@@ -203,7 +228,10 @@
             lhs[group, at:at + lon_here * PAD] = high
             lhs[group, rows + at:rows + at + lon_here * PAD] = low
 
-        def sample(nb, carry):
+    num_copies = {}
+
+    def sample(s, part):
+        def one_step(nb, carry):
             at = pl.ds(pl.multiple_of(nb * NB, NB), NB)
             hot = onehot[:, at]
             lon_ids = jnp.broadcast_to(lon_of[:, at], (PAD, NB))
@@ -227,16 +255,36 @@
             nums[s, lev, :, at] = jnp.sum(terms, axis=0, keepdims=True)
             return carry
 
-        lax.fori_loop(0, snd // NB, sample, 0)
-        copies = []
+        lax.fori_loop(part * steps // 2, (part + 1) * steps // 2, one_step, 0)
+        at = pl.ds(part * (snd // 2), snd // 2)
+        num_copies[(s, part)] = []
         for r, peer in enumerate(peers):
             copy = remote(
-                nums.at[s, lev], nums.at[s, lev],
-                n_send.at[s, r], n_recv.at[s, r], (me, peer),
+                nums.at[s, lev, :, at], nums.at[s, lev, :, at],
+                n_send.at[s, part, r], n_recv.at[s, part, r], (me, peer),
             )
             copy.start()
-            copies.append(copy)
-        halos[("n", s)] = copies
+            num_copies[(s, part)].append(copy)
+
+    mix_levels(0)
+    forward(0, 0)
+    out[0] = gathered[0, 0]
+    forward(0, 1)
+    mix_levels(1)
+    forward(1, 0)
+    out[1] = gathered[1, 0]
+    for p in range(2, hops + 1):
+        forward(0, p)
+        if p < hops:
+            forward(1, p - 1)
+    load_columns(0)
+    sample(0, 0)
+    forward(1, hops - 1)
+    sample(0, 1)
+    forward(1, hops)
+    load_columns(1)
+    sample(1, 0)
+    sample(1, 1)
 
     for copy in den_copies:
         copy.wait_recv()
@@ -245,19 +293,27 @@
         den = den + dens[z]
     in_use = lax.broadcasted_iota(jnp.int32, (1, snd), 1) < counts[0]
     for s in range(scen):
-        for copy in halos[("n", s)]:
-            copy.wait_recv()
+        for part in range(2):
+            for copy in num_copies[(s, part)]:
+                copy.wait_recv()
+            pending.extend(num_copies[(s, part)])
         num = nums[s, 0]
         for z in range(1, nlev):
             num = num + nums[s, z]
         evolved[s] = jnp.where(in_use, num / den, 0.0)
-        pending.extend(halos[("n", s)])
     pending.extend(den_copies)
-    for s in range(scen):
-        for step_copies in routes[s]:
-            pending.extend(copy for _, copy in step_copies)
     for copy in pending:
         copy.wait_send()
+    for s in range(scen):
+        @pl.when(is_end)
+        def _():
+            raw_copy(s, 2, nlev - 1 - mate).wait_send()
+            raw_copy(s, 0, mate).wait_send()
+
+        @pl.when(jnp.logical_not(is_end))
+        def _():
+            raw_copy(s, 1, nlev - 1 - lev).wait_send()
+            mixed_copy(s).wait_send()
 
 
 def body(
@@ -267,19 +323,21 @@
     snd = column.shape[0]
     tiles, nlev = lax.axis_size("tile"), lax.axis_size("lev")
     lev = lax.axis_index("lev")
-    rows = lax.dynamic_slice_in_dim(mixing, lev * lev_here, lev_here, 0)
-    rows = rows.reshape(lev_here, nlev, lev_here)
-    rows = jnp.pad(rows, ((0, PAD - lev_here), (0, 0), (0, KPAD - lev_here)))
-    rows = rows.reshape(PAD, nlev * KPAD)
+    first = lev // 2 * 2 * lev_here
+    rows = lax.dynamic_slice_in_dim(mixing, first, 2 * lev_here, 0)
+    rows = rows.reshape(2, lev_here, nlev, lev_here)
+    rows = jnp.pad(rows, ((0, 0), (0, PAD - lev_here), (0, 0), (0, KPAD - lev_here)))
+    rows = rows.reshape(2, 1, PAD, nlev * KPAD)
     high = lax.reduce_precision(rows, 8, 7)
     low = rows - high
     mix = jnp.concatenate(
         [
-            jnp.concatenate([high, high], axis=1),
-            jnp.concatenate([low, jnp.zeros_like(low)], axis=1),
+            jnp.concatenate([high, high], axis=3),
+            jnp.concatenate([low, jnp.zeros_like(low)], axis=3),
         ],
-        axis=0,
-    ).astype(jnp.bfloat16)
+        axis=1,
+    )
+    mix = mix.reshape(4 * PAD, 2 * nlev * KPAD).astype(jnp.bfloat16)
     f32, bf16 = jnp.float32, jnp.bfloat16
     block = (lev_here, nlat)
     dma = pltpu.SemaphoreType.DMA
@@ -299,6 +357,7 @@
             pltpu.VMEM((NSUB, scen) + block, f32),
             pltpu.VMEM(block, f32),
             pltpu.VMEM((scen, nlev, lon_here) + block, f32),
+            pltpu.VMEM((scen, lon_here) + block, f32),
             pltpu.VMEM((2 * nlev * KPAD, nlat), bf16),
             pltpu.VMEM((scen, tiles, lon_here) + block, f32),
             pltpu.VMEM((groups, 2 * GROUP * lon_here * PAD, nlat), bf16),
@@ -311,12 +370,14 @@
             dma((NSUB, scen, 2)),
             dma((NSUB, scen, 2)),
             dma((2,)),
-            dma((scen, nlev - 1)),
-            dma((scen, nlev - 1)),
+            dma((scen, 4)),
+            dma((scen, 4)),
             dma((scen, tiles)),
             dma((scen, tiles)),
-            dma((scen + 1, nlev - 1)),
-            dma((scen + 1, nlev - 1)),
+            dma((scen, 2, nlev - 1)),
+            dma((scen, 2, nlev - 1)),
+            dma((nlev - 1,)),
+            dma((nlev - 1,)),
         ],
         compiler_params=pltpu.CompilerParams(
             collective_id=0, has_side_effects=True, vmem_limit_bytes=56 * 2**20

time: 67.9 us -> 58 us (0.85)
  Pallas kernels: 61 us -> 51.2 us
    pallas_call x1, Pallas kernels: 61 us -> 51.2 us  [body(): pl.pallas_call(functools.partial(kernel_body, (scen, lev_here, lon_here,...]
where the time goes in v2:
time: 58 us; the launch traced here: 57.7 us
  Pallas kernels  51.2 us (88%)
  local copies, waits for them, and re-layouts  4.51 us (8%)
  between operations  1.36 us (2%)
  other arithmetic  0.63 us (1%)
    pallas_call x1, Pallas kernels, body(): pl.pallas_call(functools.partial(kernel_body, (scen, lev_here, lon_here,...  51.2 us
    unnamed x13, local copies, waits for them, and re-layouts  3.58 us

profile of v2, /device:TPU:0, one launch (start us, length us, event | category | flops | bytes accessed | tf_op | source)
XLA Modules:
  0.0 57.7 jit_solution(14356289888253866005)
XLA Ops:
  0.6 0.0 copy-start
  1.3 0.1 copy-done
  1.4 0.1 reshape.40
  1.5 0.0 copy-start.1
  1.6 0.1 reshape.41
  1.7 0.6 %fusion.1 = bf16[2,2,24,256]{3,2,1,0:T(8,128)(2,1)} fusion(bf16[2,1,24,128]{3,2,1,0:T(8,128)(2,1)S(1)} %get-tuple-element.9, bf16[2,1,24,128]{3,2,1,0:T(8,128)(2,1)S(1)} %get-tuple-element.8), kind=kLoop, calls=%fused_computation.5 | loop fusion | flops 196608 | bytes 73728 | tf_op jit(solution)/shard_map/concatenate | solution.py:333
  2.3 0.2 copy-done.1
  2.5 0.0 copy-start.2
  2.5 0.0 copy-start.3
  2.5 0.7 %copy.21 = f32[2,18,2,512]{3,1,2,0:T(8,128)} copy(f32[2,18,2,512]{3,2,1,0:T(2,128)S(1)} %copy-done.1) | data formatting | bytes 294912 | tf_op args[0]
  3.2 0.2 copy-done.2
  3.3 0.1 copy-done.3
  3.4 0.7 %copy_bitcast_fusion.1 = (f32[2,18,512]{2,1,0:T(8,128)}, f32[2,18,512]{2,1,0:T(8,128)}) fusion(f32[18,2,512]{2,1,0:T(2,128)S(1)} %copy-done.2, f32[18,2,512]{2,1,0:T(2,128)S(1)} %copy-done.3), kind=kLoop, calls=%fused_computation.2 | loop fusion | bytes 294912 | tf_op jit(solution)/shard_map/transpose | solution.py:388
  4.1 51.2 %shard_map.113 = (f32[2,2,18,512]{3,2,1,0:T(8,128)}, f32[2,1,4096]{2,1,0:T(1,128)}) custom-call(f32[2,2,18,512]{3,2,1,0:T(8,128)} %bitcast.15, f32[2,18,512]{2,1,0:T(8,128)} %get-tuple-element.11.u_ref, f32[2,18,512]{2,1,0:T(8,128)} %get-tuple-element.10.v_ref, f32[2,2,512]{2,1,0:T(2,128)} %flux.1, bf16[96,256]{1,0:T(8,128)(2,1)} %bitcast.16, ...), custom_call_target="tpu_custom_call" | custom-call | tf_op jit(solution)/shard_map/pallas_call | solution.py:346
  55.4 0.0 copy-start.4
  55.4 1.7 %copy.15 = f32[2,18,2,512]{3,2,1,0:T(2,128)} copy(f32[2,18,2,512]{3,1,2,0:T(8,128)} %bitcast.17) | data formatting | bytes 294912
  57.1 0.0 copy-done.4
  57.1 0.6 %copy.22 = f32[2,1,4096]{2,0,1:T(2,128)} copy(f32[2,1,4096]{2,1,0:T(1,128)S(1)} %copy-done.4) | data formatting | bytes 65536
  (3 shorter events, 0.0 us)
Async XLA Ops:
  0.6 0.8 %copy-start = (f32[72,72]{1,0:T(8,128)S(1)}, f32[72,72]{1,0:T(8,128)}, u32[]{:S(2)}) copy-start(f32[72,72]{1,0:T(8,128)} %param.14) | copy-start | bytes 62212
  1.5 0.9 %copy-start.1 = (f32[2,18,2,512]{3,2,1,0:T(2,128)S(1)}, f32[2,18,2,512]{3,2,1,0:T(2,128)}, u32[]{:S(2)}) copy-start(f32[2,18,2,512]{3,2,1,0:T(2,128)} %param.10) | copy-start | bytes 442372
  2.5 0.9 %copy-start.2 = (f32[18,2,512]{2,1,0:T(2,128)S(1)}, f32[18,2,512]{2,1,0:T(2,128)}, u32[]{:S(2)}) copy-start(f32[18,2,512]{2,1,0:T(2,128)} %param.12) | copy-start | bytes 221188
  2.5 1.0 %copy-start.3 = (f32[18,2,512]{2,1,0:T(2,128)S(1)}, f32[18,2,512]{2,1,0:T(2,128)}, u32[]{:S(2)}) copy-start(f32[18,2,512]{2,1,0:T(2,128)} %param.11) | copy-start | bytes 221188
  55.4 1.7 %copy-start.4 = (f32[2,1,4096]{2,1,0:T(1,128)S(1)}, f32[2,1,4096]{2,1,0:T(1,128)}, u32[]{:S(2)}) copy-start(f32[2,1,4096]{2,1,0:T(1,128)} %get-tuple-element.5) | copy-start | bytes 98308

commit v3 on v2

v3 whole, which is shorter than its diff:
```python
import functools
import jax
import jax.numpy as jnp
from jax import lax
from jax.experimental import pallas as pl
from jax.experimental.pallas import tpu as pltpu
from jax.sharding import PartitionSpec as P

NSUB = 2
PAD = 24
KPAD = 32
NB = 256
CHUNKS = 4
GROUP = 8
MESH = pl.DeviceIdType.MESH


def split(x):
    high = x.astype(jnp.bfloat16)
    low = (x - high.astype(jnp.float32)).astype(jnp.bfloat16)
    return high, low


def grow(x, rows):
    return jnp.concatenate([x, jnp.zeros((rows - x.shape[0], x.shape[1]), x.dtype)], axis=0)


def flip(index, bit):
    return index + bit - 2 * bit * ((index // bit) % 2)


def substep(cells, winds, lat_winds, lat_ids):
    count = len(lat_winds)
    size = cells[0].shape[-1]
    west = [
        winds[i] * jnp.where(winds[i] > 0, cells[i], cells[i + 1]) for i in range(count + 1)
    ]
    result = []
    for i in range(count):
        centre = cells[i + 1]
        south_cells = pltpu.roll(centre, 1, 1)
        south = lat_winds[i] * jnp.where(lat_winds[i] > 0, south_cells, centre)
        south = jnp.where(lat_ids > 0, south, 0.0)
        north = pltpu.roll(south, size - 1, 1)
        result.append(centre - (west[i + 1] - west[i]) - (north - south))
    return result


def kernel_body(
    dims,
    tracer, u_ref, v_ref, flux, mix, kern, column, owner, offset, counts,
    out, evolved,
    cur, halo_w, halo_e, halo_u, mixed, mixed_in, rhs, gathered, levs, lhs, onehot, lon_of,
    weight, eff, eff_out, nums, dens,
    h_send, h_recv, u_sem, z_send, z_recv, w_send, w_recv, g_send, g_recv, n_send, n_recv,
    d_send, d_recv,
):
    scen, lev_here, lon_here, nlat, snd, tiles, nlev = dims
    me, lev = lax.axis_index("tile"), lax.axis_index("lev")
    east, west = lax.rem(me + 1, tiles), lax.rem(me + tiles - 1, tiles)
    bits = [1 << k for k in range(tiles.bit_length() - 1)]
    peers = [lax.rem(lev + r, nlev) for r in range(1, nlev)]

    barrier = pltpu.get_barrier_semaphore()
    friends = [(east, lev), (west, lev)]
    friends += [(flip(me, b), lev) for b in bits]
    friends += [(me, p) for p in peers]
    for friend in friends:
        pl.semaphore_signal(barrier, inc=1, device_id=friend, device_id_type=MESH)

    row_ids = lax.broadcasted_iota(jnp.int32, (lev_here, nlat), 0)
    lat_ids = lax.broadcasted_iota(jnp.int32, (lev_here, nlat), 1)
    bottom = jnp.logical_and(row_ids == 0, lev == 0)
    for s in range(scen):
        for i in range(lon_here):
            here = tracer[s, i]
            cur[0, s, i] = jnp.where(bottom, here + flux[s, pl.ds(i, 1)], here)
    pl.semaphore_wait(barrier, len(friends))

    def remote(src, dst, send, recv, device):
        return pltpu.make_async_remote_copy(
            src_ref=src, dst_ref=dst, send_sem=send, recv_sem=recv,
            device_id=device, device_id_type=MESH,
        )

    pending = []

    def send_halo(step, s):
        to_east = remote(
            cur.at[step, s, lon_here - 1], halo_w.at[step, s],
            h_send.at[step, s, 0], h_recv.at[step, s, 0], (east, lev),
        )
        to_west = remote(
            cur.at[step, s, 0], halo_e.at[step, s],
            h_send.at[step, s, 1], h_recv.at[step, s, 1], (west, lev),
        )
        to_east.start()
        to_west.start()
        pending.extend([to_east, to_west])
        return to_east, to_west

    u_copy = remote(u_ref.at[0], halo_u, u_sem.at[0], u_sem.at[1], (west, lev))
    u_copy.start()
    pending.append(u_copy)
    halos = {(0, s): send_halo(0, s) for s in range(scen)}

    steps = snd // NB
    half, parity = lev // 2, lev % 2
    is_end = half == parity
    is_inner = jnp.logical_not(is_end)
    mate = half * 2 + 1 - parity
    level_ids = lev * lev_here + lax.broadcasted_iota(jnp.int32, (lev_here, NB), 0)
    width = snd // CHUNKS

    def weigh(nb, carry):
        at = pl.ds(pl.multiple_of(nb * NB, NB), NB)
        used_weight = jnp.where(level_ids >= offset[:, at], kern[:, at], 0.0)
        weight[lev, :, at] = used_weight
        dens[lev, :, at] = jnp.sum(used_weight, axis=0, keepdims=True)
        return carry

    lax.fori_loop(0, steps, weigh, 0)

    def weight_copy(c, k, to):
        part = weight.at[lev, :, pl.ds(c * width, width)]
        return remote(part, part, w_send.at[c, k], w_recv.at[c, k], (me, to))

    def eff_copy(c):
        at = pl.ds(c * width, width)
        return remote(
            eff_out.at[:, at], eff.at[:, at], w_send.at[c, 3], w_recv.at[c, 3], (me, mate)
        )

    def raw_copy(s, k, to):
        return remote(
            levs.at[s, lev], levs.at[s, lev], z_send.at[s, k], z_recv.at[s, k], (me, to)
        )

    def mixed_copy(s):
        return remote(
            mixed.at[s], mixed_in.at[s], z_send.at[s, 3], z_recv.at[s, 3], (me, mate)
        )

    @pl.when(is_end)
    def _():
        for c in range(CHUNKS):
            weight_copy(c, 2, nlev - 1 - mate).start()
            weight_copy(c, 0, mate).start()

    @pl.when(is_inner)
    def _():
        for c in range(CHUNKS):
            weight_copy(c, 1, nlev - 1 - lev).start()

    den_copies = []
    for r, peer in enumerate(peers):
        copy = remote(
            dens.at[lev], dens.at[lev],
            d_send.at[r], d_recv.at[r], (me, peer),
        )
        copy.start()
        den_copies.append(copy)

    lat_rows = lax.broadcasted_iota(jnp.int32, (nlat, NB), 0)

    def prepare(nb, carry):
        at = pl.ds(pl.multiple_of(nb * NB, NB), NB)
        col = column[:, at]
        lon_in = col // nlat
        lat = col - lon_in * nlat
        onehot[:, at] = (lat_rows == lat).astype(jnp.float32).astype(jnp.bfloat16)
        lon_of[:, at] = owner[:, at] * lon_here + lon_in
        return carry

    def mix_blocks(kind, blocks):
        for z, block in enumerate(blocks):
            high, low = split(grow(block, KPAD))
            rhs[z * KPAD:(z + 1) * KPAD] = high
            rhs[(nlev + z) * KPAD:(nlev + z + 1) * KPAD] = low
        both = jnp.dot(mix[kind], rhs[...], preferred_element_type=jnp.float32)
        first = both[0:PAD] + both[PAD:2 * PAD]
        second = both[2 * PAD:3 * PAD] + both[3 * PAD:4 * PAD]
        own = jnp.where(parity == 0, first, second)
        other = jnp.where(parity == 0, second, first)
        return own[0:lev_here], other[0:lev_here]

    def mix_weights(c):
        @pl.when(is_inner)
        def _():
            for k in range(3):
                weight_copy(c, k, mate).wait_recv()
            for n in range(c * width, (c + 1) * width, nlat):
                at = pl.ds(n, nlat)
                own, other = mix_blocks(1, [weight[z, :, at] for z in range(nlev)])
                eff[:, at] = own
                eff_out[:, at] = other
            eff_copy(c).start()

    def wait_weights(c):
        @pl.when(is_end)
        def _():
            eff_copy(c).wait_recv()

    def mix_levels(s):
        @pl.when(is_inner)
        def _():
            for k in range(3):
                raw_copy(s, k, mate).wait_recv()
            for i in range(lon_here):
                own, other = mix_blocks(0, [levs[s, z, i] for z in range(nlev)])
                out[s, i] = own
                mixed[s, i] = other
            mixed_copy(s).start()

    orders = [bits[::-1], bits[-2:0:-1] + bits[-1:] + bits[:1]]

    def masks_at(s, p):
        held = [0]
        for bit in orders[s % 2][:p]:
            held = held + [m + bit for m in held]
        return held

    def block_copy(s, m, bit):
        return remote(
            gathered.at[s, m], gathered.at[s, m + bit],
            g_send.at[s, m + bit], g_recv.at[s, m + bit], (flip(me, bit), lev),
        )

    def forward(s, p):
        order = orders[s % 2]
        fresh = [0] if p == 0 else [m + order[p - 1] for m in masks_at(s, p - 1)]
        for m in fresh:
            if p > 0:
                block_copy(s, m - order[p - 1], order[p - 1]).wait_recv()
            for bit in order[p:]:
                copy = block_copy(s, m, bit)
                copy.start()
                pending.append(copy)

        for m in fresh:
            load_columns(s, m)

    rows = GROUP * lon_here * PAD
    hops = len(bits)

    def load_columns(s, m):
        blocks = [grow(gathered[s, m, i], PAD) for i in range(lon_here)]
        high, low = split(jnp.concatenate(blocks, axis=0))
        at = m % GROUP * lon_here * PAD
        lhs[s, m // GROUP, at:at + lon_here * PAD, 0:nlat] = high
        lhs[s, m // GROUP, at:at + lon_here * PAD, nlat:2 * nlat] = low

    num_copies = {}

    def sample(s, part):
        def one_step(nb, carry):
            at = pl.ds(pl.multiple_of(nb * NB, NB), NB)
            hot = onehot[:, at]
            twice = jnp.concatenate([hot, hot], axis=0)
            lon_ids = jnp.broadcast_to(lon_of[:, at], (PAD, NB))

            def one_group(group, acc):
                found = jnp.dot(lhs[s, group], twice, preferred_element_type=jnp.float32)
                for inner in range(GROUP):
                    tile = jnp.bitwise_xor(me, group * GROUP + inner)
                    for i in range(lon_here):
                        r = (inner * lon_here + i) * PAD
                        block = found[r:r + PAD]
                        acc = jnp.where(lon_ids == tile * lon_here + i, block, acc)
                return acc

            acc = jnp.zeros((PAD, NB), jnp.float32)
            if tiles == GROUP:
                acc = one_group(0, acc)
            else:
                acc = lax.fori_loop(0, tiles // GROUP, one_group, acc)
            terms = acc[0:lev_here] * eff[:, at]
            nums[s, lev, :, at] = jnp.sum(terms, axis=0, keepdims=True)
            return carry

        lax.fori_loop(part * steps // 2, (part + 1) * steps // 2, one_step, 0)
        at = pl.ds(part * (snd // 2), snd // 2)
        num_copies[(s, part)] = []
        for r, peer in enumerate(peers):
            copy = remote(
                nums.at[s, lev, :, at], nums.at[s, lev, :, at],
                n_send.at[s, part, r], n_recv.at[s, part, r], (me, peer),
            )
            copy.start()
            num_copies[(s, part)].append(copy)

    lax.fori_loop(0, steps // 2, prepare, 0)
    u_copy.wait_recv()
    for step in range(NSUB):
        for s in range(scen):
            for copy in halos[(step, s)]:
                copy.wait_recv()
            cells = [halo_w[step, s]] + [cur[step, s, i] for i in range(lon_here)]
            cells.append(halo_e[step, s])
            winds = [u_ref[i] for i in range(lon_here)] + [halo_u[...]]
            new = substep(cells, winds, [v_ref[i] for i in range(lon_here)], lat_ids)
            if step < NSUB - 1:
                for i in range(lon_here):
                    cur[step + 1, s, i] = new[i]
                halos[(step + 1, s)] = send_halo(step + 1, s)
                continue
            for i in range(lon_here):
                gathered[s, 0, i] = new[i]
                levs[s, lev, i] = new[i]

            forward(s, 0)

            @pl.when(is_end)
            def _():
                raw_copy(s, 2, nlev - 1 - mate).start()
                raw_copy(s, 0, mate).start()

            @pl.when(is_inner)
            def _():
                raw_copy(s, 1, nlev - 1 - lev).start()
        if step == 0:
            lax.fori_loop(steps // 2, steps, prepare, 0)

    mix_weights(0)
    forward(0, 1)
    forward(1, 1)
    mix_weights(1)
    for p in range(2, hops):
        forward(0, p)
        if p < hops - 1:
            forward(1, p)
    mix_weights(2)
    forward(0, hops)
    forward(1, hops - 1)
    mix_weights(3)
    wait_weights(0)
    wait_weights(1)
    sample(0, 0)
    forward(1, hops)
    wait_weights(2)
    wait_weights(3)
    sample(0, 1)
    sample(1, 0)
    mix_levels(0)
    sample(1, 1)
    mix_levels(1)

    for copy in den_copies:
        copy.wait_recv()
    den = dens[0]
    for z in range(1, nlev):
        den = den + dens[z]
    in_use = lax.broadcasted_iota(jnp.int32, (1, snd), 1) < counts[0]
    for s in range(scen):
        for part in range(2):
            for copy in num_copies[(s, part)]:
                copy.wait_recv()
            pending.extend(num_copies[(s, part)])
        num = nums[s, 0]
        for z in range(1, nlev):
            num = num + nums[s, z]
        evolved[s] = jnp.where(in_use, num / den, 0.0)
    pending.extend(den_copies)
    for copy in pending:
        copy.wait_send()
    for s in range(scen):
        @pl.when(is_end)
        def _():
            mixed_copy(s).wait_recv()
            out[s] = mixed_in[s]
            raw_copy(s, 2, nlev - 1 - mate).wait_send()
            raw_copy(s, 0, mate).wait_send()

        @pl.when(is_inner)
        def _():
            raw_copy(s, 1, nlev - 1 - lev).wait_send()
            mixed_copy(s).wait_send()
    for c in range(CHUNKS):
        @pl.when(is_end)
        def _():
            weight_copy(c, 2, nlev - 1 - mate).wait_send()
            weight_copy(c, 0, mate).wait_send()

        @pl.when(is_inner)
        def _():
            weight_copy(c, 1, nlev - 1 - lev).wait_send()
            eff_copy(c).wait_send()


def body(
    tracer, u_courant, v_courant, surface_flux, mixing, kernel, column, owner_tile, offset, counts
):
    scen, lev_here, lon_here, nlat = tracer.shape
    snd = column.shape[0]
    tiles, nlev = lax.axis_size("tile"), lax.axis_size("lev")
    lev = lax.axis_index("lev")
    first = lev // 2 * 2 * lev_here
    rows = lax.dynamic_slice_in_dim(
        jnp.stack([mixing, mixing.T]), first, 2 * lev_here, 1
    )
    rows = rows.reshape(2, 2, lev_here, nlev, lev_here)
    rows = jnp.pad(rows, ((0, 0), (0, 0), (0, PAD - lev_here), (0, 0), (0, KPAD - lev_here)))
    rows = rows.reshape(2, 2, 1, PAD, nlev * KPAD)
    high = lax.reduce_precision(rows, 8, 7)
    low = rows - high
    mix = jnp.concatenate(
        [
            jnp.concatenate([high, high], axis=4),
            jnp.concatenate([low, jnp.zeros_like(low)], axis=4),
        ],
        axis=2,
    )
    mix = mix.reshape(2, 4 * PAD, 2 * nlev * KPAD).astype(jnp.bfloat16)
    f32, bf16 = jnp.float32, jnp.bfloat16
    block = (lev_here, nlat)
    dma = pltpu.SemaphoreType.DMA
    vmem = pl.BlockSpec(memory_space=pltpu.VMEM)
    groups = tiles // GROUP
    out, evolved = pl.pallas_call(
        functools.partial(kernel_body, (scen, lev_here, lon_here, nlat, snd, tiles, nlev)),
        out_shape=(
            jax.ShapeDtypeStruct((scen, lon_here) + block, f32),
            jax.ShapeDtypeStruct((scen, 1, snd), f32),
        ),
        in_specs=[vmem] * 9 + [pl.BlockSpec(memory_space=pltpu.SMEM)],
        out_specs=(vmem, vmem),
        scratch_shapes=[
            pltpu.VMEM((NSUB, scen, lon_here) + block, f32),
            pltpu.VMEM((NSUB, scen) + block, f32),
            pltpu.VMEM((NSUB, scen) + block, f32),
            pltpu.VMEM(block, f32),
            pltpu.VMEM((scen, lon_here) + block, f32),
            pltpu.VMEM((scen, lon_here) + block, f32),
            pltpu.VMEM((2 * nlev * KPAD, nlat), bf16),
            pltpu.VMEM((scen, tiles, lon_here) + block, f32),
            pltpu.VMEM((scen, nlev, lon_here) + block, f32),
            pltpu.VMEM((scen, groups, GROUP * lon_here * PAD, 2 * nlat), bf16),
            pltpu.VMEM((nlat, snd), bf16),
            pltpu.VMEM((1, snd), jnp.int32),
            pltpu.VMEM((nlev, lev_here, snd), f32),
            pltpu.VMEM((lev_here, snd), f32),
            pltpu.VMEM((lev_here, snd), f32),
            pltpu.VMEM((scen, nlev, 1, snd), f32),
            pltpu.VMEM((nlev, 1, snd), f32),
            dma((NSUB, scen, 2)),
            dma((NSUB, scen, 2)),
            dma((2,)),
            dma((scen, 4)),
            dma((scen, 4)),
            dma((CHUNKS, 4)),
            dma((CHUNKS, 4)),
            dma((scen, tiles)),
            dma((scen, tiles)),
            dma((scen, 2, nlev - 1)),
            dma((scen, 2, nlev - 1)),
            dma((nlev - 1,)),
            dma((nlev - 1,)),
        ],
        compiler_params=pltpu.CompilerParams(
            collective_id=0, has_side_effects=True, vmem_limit_bytes=56 * 2**20
        ),
    )(
        tracer.transpose(0, 2, 1, 3),
        u_courant.transpose(1, 0, 2),
        v_courant.transpose(1, 0, 2),
        surface_flux,
        mix,
        kernel,
        column[None],
        owner_tile[None],
        offset[None],
        counts,
    )
    return out.transpose(0, 2, 1, 3), evolved[:, 0]


def solution(mesh):
    in_specs = (
        P(None, "lev", "tile", None),
        P("lev", "tile", None),
        P("lev", "tile", None),
        P(None, "tile", None),
        P(),
        P("lev", "tile"),
        P("tile"),
        P("tile"),
        P("tile"),
        P("tile"),
    )
    out_specs = (P(None, "lev", "tile", None), P(None, "tile"))
    return jax.shard_map(body, mesh=mesh, in_specs=in_specs, out_specs=out_specs, check_vma=False)
```

time: 58 us -> 52.1 us (0.90)
  Pallas kernels: 51.2 us -> 45 us
    pallas_call x1, Pallas kernels: 51.2 us -> 45 us  [body(): pl.pallas_call(functools.partial(kernel_body, (scen, lev_here, lon_here,...]
    unnamed x13 -> x14, local copies, waits for them, and re-layouts: 3.58 us -> 3.77 us
where the time goes in v3:
time: 52.1 us; the launch traced here: 51.8 us
  Pallas kernels  45 us (86%)
  local copies, waits for them, and re-layouts  4.83 us (9%)
  between operations  1.37 us (3%)
  other arithmetic  0.67 us (1%)
    pallas_call x1, Pallas kernels, body(): pl.pallas_call(functools.partial(kernel_body, (scen, lev_here, lon_here,...  45 us
    unnamed x14, local copies, waits for them, and re-layouts  3.77 us

profile of v3, /device:TPU:0, one launch (start us, length us, event | category | flops | bytes accessed | tf_op | source)
XLA Modules:
  0.0 51.8 jit_solution(6406672238689615511)
XLA Ops:
  0.6 0.0 copy-start
  1.3 0.1 copy-done
  1.4 0.1 copy.19
  1.5 0.1 reshape.40
  1.7 0.2 reshape.41
  1.9 0.0 copy-start.1
  1.9 0.6 %fusion.1 = bf16[2,2,2,24,256]{4,3,2,1,0:T(8,128)(2,1)} fusion(bf16[2,2,1,24,128]{4,3,2,1,0:T(8,128)(2,1)S(1)} %get-tuple-element.11, bf16[2,2,1,24,128]{4,3,2,1,0:T(8,128)(2,1)S(1)} %get-tuple-element.10), kind=kLoop, calls=%fused_computation.3 | loop fusion | flops 393216 | bytes 147456 | tf_op jit(solution)/shard_map/concatenate | solution.py:406
  2.6 0.3 copy-done.1
  2.8 0.0 copy-start.2
  2.8 0.0 copy-start.3
  2.8 0.7 %copy.31 = f32[2,18,2,512]{3,1,2,0:T(8,128)} copy(f32[2,18,2,512]{3,2,1,0:T(2,128)S(1)} %copy-done.1) | data formatting | bytes 294912 | tf_op args[0]
  3.5 0.2 copy-done.2
  3.7 0.1 copy-done.3
  3.8 0.7 %copy_bitcast_fusion.1 = (f32[2,18,512]{2,1,0:T(8,128)}, f32[2,18,512]{2,1,0:T(8,128)}) fusion(f32[18,2,512]{2,1,0:T(2,128)S(1)} %copy-done.2, f32[18,2,512]{2,1,0:T(2,128)S(1)} %copy-done.3), kind=kLoop, calls=%fused_computation.4 | loop fusion | bytes 294912 | tf_op jit(solution)/shard_map/transpose | solution.py:465
  4.5 45.0 %shard_map.113 = (f32[2,2,18,512]{3,2,1,0:T(8,128)}, f32[2,1,4096]{2,1,0:T(1,128)}) custom-call(f32[2,2,18,512]{3,2,1,0:T(8,128)} %bitcast.23, f32[2,18,512]{2,1,0:T(8,128)} %get-tuple-element.13.u_ref, f32[2,18,512]{2,1,0:T(8,128)} %get-tuple-element.12.v_ref, f32[2,2,512]{2,1,0:T(2,128)} %flux.1, bf16[2,96,256]{2,1,0:T(8,128)(2,1)} %bitcast.24, ...), custom_call_target="tpu_custom_call" | custom-call | tf_op jit(solution)/shard_map/pallas_call | solution.py:419
  49.5 0.0 copy-start.4
  49.5 1.7 %copy.23 = f32[2,18,2,512]{3,2,1,0:T(2,128)} copy(f32[2,18,2,512]{3,1,2,0:T(8,128)} %bitcast.25) | data formatting | bytes 294912
  51.2 0.0 copy-done.4
  51.2 0.6 %copy.32 = f32[2,1,4096]{2,0,1:T(2,128)} copy(f32[2,1,4096]{2,1,0:T(1,128)S(1)} %copy-done.4) | data formatting | bytes 65536
  (4 shorter events, 0.1 us)
Async XLA Ops:
  0.6 0.8 %copy-start = (f32[72,72]{1,0:T(8,128)S(1)}, f32[72,72]{1,0:T(8,128)}, u32[]{:S(2)}) copy-start(f32[72,72]{1,0:T(8,128)} %param.14) | copy-start | bytes 62212
  1.9 0.9 %copy-start.1 = (f32[2,18,2,512]{3,2,1,0:T(2,128)S(1)}, f32[2,18,2,512]{3,2,1,0:T(2,128)}, u32[]{:S(2)}) copy-start(f32[2,18,2,512]{3,2,1,0:T(2,128)} %param.10) | copy-start | bytes 442372
  2.8 0.9 %copy-start.2 = (f32[18,2,512]{2,1,0:T(2,128)S(1)}, f32[18,2,512]{2,1,0:T(2,128)}, u32[]{:S(2)}) copy-start(f32[18,2,512]{2,1,0:T(2,128)} %param.12) | copy-start | bytes 221188
  2.8 1.0 %copy-start.3 = (f32[18,2,512]{2,1,0:T(2,128)S(1)}, f32[18,2,512]{2,1,0:T(2,128)}, u32[]{:S(2)}) copy-start(f32[18,2,512]{2,1,0:T(2,128)} %param.11) | copy-start | bytes 221188
  49.5 1.7 %copy-start.4 = (f32[2,1,4096]{2,1,0:T(1,128)S(1)}, f32[2,1,4096]{2,1,0:T(1,128)}, u32[]{:S(2)}) copy-start(f32[2,1,4096]{2,1,0:T(1,128)} %get-tuple-element.5) | copy-start | bytes 98308

commit v4 on v3

--- a/solution.py
+++ b/solution.py
@@ -11,7 +11,7 @@
 KPAD = 32
 NB = 256
 CHUNKS = 4
-GROUP = 8
+GROUP = 4
 MESH = pl.DeviceIdType.MESH
 
 
@@ -51,7 +51,7 @@
     tracer, u_ref, v_ref, flux, mix, kern, column, owner, offset, counts,
     out, evolved,
     cur, halo_w, halo_e, halo_u, mixed, mixed_in, rhs, gathered, levs, lhs, onehot, lon_of,
-    weight, eff, eff_out, nums, dens,
+    weight, eff, eff_out, found_at, nums, dens,
     h_send, h_recv, u_sem, z_send, z_recv, w_send, w_recv, g_send, g_recv, n_send, n_recv,
     d_send, d_recv,
 ):
@@ -240,45 +240,56 @@
         for m in fresh:
             load_columns(s, m)
 
-    rows = GROUP * lon_here * PAD
-    hops = len(bits)
+    hops = len(bits) - 1
+
+    def arrivals(s):
+        return [m + c for m in masks_at(s, hops) for c in range(2)]
 
     def load_columns(s, m):
         blocks = [grow(gathered[s, m, i], PAD) for i in range(lon_here)]
         high, low = split(jnp.concatenate(blocks, axis=0))
-        at = m % GROUP * lon_here * PAD
-        lhs[s, m // GROUP, at:at + lon_here * PAD, 0:nlat] = high
-        lhs[s, m // GROUP, at:at + lon_here * PAD, nlat:2 * nlat] = low
+        place = arrivals(s).index(m)
+        at = place % GROUP * lon_here * PAD
+        lhs[s, place // GROUP, at:at + lon_here * PAD, 0:nlat] = high
+        lhs[s, place // GROUP, at:at + lon_here * PAD, nlat:2 * nlat] = low
+
+    groups = tiles // GROUP
 
     num_copies = {}
 
-    def sample(s, part):
+    def search(s, group, low, high):
+        slots = arrivals(s)[group * GROUP:(group + 1) * GROUP]
+        for m in slots:
+            if m % 2 == 1:
+                block_copy(s, m - 1, 1).wait_recv()
+                load_columns(s, m)
+        resume(s, group, low, high)
+
+    def resume(s, group, low, high):
+        slots = arrivals(s)[group * GROUP:(group + 1) * GROUP]
+
         def one_step(nb, carry):
             at = pl.ds(pl.multiple_of(nb * NB, NB), NB)
             hot = onehot[:, at]
             twice = jnp.concatenate([hot, hot], axis=0)
             lon_ids = jnp.broadcast_to(lon_of[:, at], (PAD, NB))
-
-            def one_group(group, acc):
-                found = jnp.dot(lhs[s, group], twice, preferred_element_type=jnp.float32)
-                for inner in range(GROUP):
-                    tile = jnp.bitwise_xor(me, group * GROUP + inner)
-                    for i in range(lon_here):
-                        r = (inner * lon_here + i) * PAD
-                        block = found[r:r + PAD]
-                        acc = jnp.where(lon_ids == tile * lon_here + i, block, acc)
-                return acc
-
-            acc = jnp.zeros((PAD, NB), jnp.float32)
-            if tiles == GROUP:
-                acc = one_group(0, acc)
+            found = jnp.dot(lhs[s, group], twice, preferred_element_type=jnp.float32)
+            acc = jnp.zeros((PAD, NB), jnp.float32) if group == 0 else found_at[s, :, at]
+            for inner, m in enumerate(slots):
+                tile = jnp.bitwise_xor(me, m)
+                for i in range(lon_here):
+                    r = (inner * lon_here + i) * PAD
+                    acc = jnp.where(lon_ids == tile * lon_here + i, found[r:r + PAD], acc)
+            if group < groups - 1:
+                found_at[s, :, at] = acc
             else:
-                acc = lax.fori_loop(0, tiles // GROUP, one_group, acc)
-            terms = acc[0:lev_here] * eff[:, at]
-            nums[s, lev, :, at] = jnp.sum(terms, axis=0, keepdims=True)
+                terms = acc[0:lev_here] * eff[:, at]
+                nums[s, lev, :, at] = jnp.sum(terms, axis=0, keepdims=True)
             return carry
 
-        lax.fori_loop(part * steps // 2, (part + 1) * steps // 2, one_step, 0)
+        lax.fori_loop(low, high, one_step, 0, unroll=2)
+
+    def send_nums(s, part):
         at = pl.ds(part * (snd // 2), snd // 2)
         num_copies[(s, part)] = []
         for r, peer in enumerate(peers):
@@ -324,26 +335,33 @@
     mix_weights(0)
     forward(0, 1)
     forward(1, 1)
+    search(0, 0, 0, steps)
+    forward(0, 2)
     mix_weights(1)
-    for p in range(2, hops):
+    search(1, 0, 0, steps)
+    forward(1, 2)
+    for p in range(3, hops + 1):
         forward(0, p)
-        if p < hops - 1:
-            forward(1, p)
+        forward(1, p)
     mix_weights(2)
-    forward(0, hops)
-    forward(1, hops - 1)
+    for group in range(1, groups - 1):
+        search(0, group, 0, steps)
+        search(1, group, 0, steps)
     mix_weights(3)
     wait_weights(0)
     wait_weights(1)
-    sample(0, 0)
-    forward(1, hops)
+    search(0, groups - 1, 0, steps // 2)
+    send_nums(0, 0)
     wait_weights(2)
     wait_weights(3)
-    sample(0, 1)
-    sample(1, 0)
+    resume(0, groups - 1, steps // 2, steps)
+    send_nums(0, 1)
     mix_levels(0)
-    sample(1, 1)
+    search(1, groups - 1, 0, steps // 2)
+    send_nums(1, 0)
     mix_levels(1)
+    resume(1, groups - 1, steps // 2, steps)
+    send_nums(1, 1)
 
     for copy in den_copies:
         copy.wait_recv()
@@ -440,6 +458,7 @@
             pltpu.VMEM((nlev, lev_here, snd), f32),
             pltpu.VMEM((lev_here, snd), f32),
             pltpu.VMEM((lev_here, snd), f32),
+            pltpu.VMEM((scen, PAD, snd), f32),
             pltpu.VMEM((scen, nlev, 1, snd), f32),
             pltpu.VMEM((nlev, 1, snd), f32),
             dma((NSUB, scen, 2)),

time: 52.1 us -> 50.4 us (0.967)
  Pallas kernels: 45 us -> 43.3 us
    pallas_call x1, Pallas kernels: 45 us -> 43.3 us  [body(): pl.pallas_call(functools.partial(kernel_body, (scen, lev_here, lon_here,...]
where the time goes in v4:
time: 50.4 us; the launch traced here: 50.1 us
  Pallas kernels  43.3 us (86%)
  local copies, waits for them, and re-layouts  4.83 us (10%)
  between operations  1.37 us (3%)
  other arithmetic  0.67 us (1%)
    pallas_call x1, Pallas kernels, body(): pl.pallas_call(functools.partial(kernel_body, (scen, lev_here, lon_here,...  43.3 us
    unnamed x14, local copies, waits for them, and re-layouts  3.77 us

profile of v4, /device:TPU:0, one launch (start us, length us, event | category | flops | bytes accessed | tf_op | source)
XLA Modules:
  0.0 50.1 jit_solution(4583770387821251620)
XLA Ops:
  0.6 0.0 copy-start
  1.3 0.1 copy-done
  1.4 0.1 copy.19
  1.5 0.1 reshape.40
  1.7 0.2 reshape.41
  1.9 0.0 copy-start.1
  1.9 0.6 %fusion.1 = bf16[2,2,2,24,256]{4,3,2,1,0:T(8,128)(2,1)} fusion(bf16[2,2,1,24,128]{4,3,2,1,0:T(8,128)(2,1)S(1)} %get-tuple-element.11, bf16[2,2,1,24,128]{4,3,2,1,0:T(8,128)(2,1)S(1)} %get-tuple-element.10), kind=kLoop, calls=%fused_computation.3 | loop fusion | flops 393216 | bytes 147456 | tf_op jit(solution)/shard_map/concatenate | solution.py:424
  2.6 0.3 copy-done.1
  2.8 0.0 copy-start.2
  2.8 0.0 copy-start.3
  2.8 0.7 %copy.31 = f32[2,18,2,512]{3,1,2,0:T(8,128)} copy(f32[2,18,2,512]{3,2,1,0:T(2,128)S(1)} %copy-done.1) | data formatting | bytes 294912 | tf_op args[0]
  3.5 0.2 copy-done.2
  3.7 0.1 copy-done.3
  3.8 0.7 %copy_bitcast_fusion.1 = (f32[2,18,512]{2,1,0:T(8,128)}, f32[2,18,512]{2,1,0:T(8,128)}) fusion(f32[18,2,512]{2,1,0:T(2,128)S(1)} %copy-done.2, f32[18,2,512]{2,1,0:T(2,128)S(1)} %copy-done.3), kind=kLoop, calls=%fused_computation.4 | loop fusion | bytes 294912 | tf_op jit(solution)/shard_map/transpose | solution.py:484
  4.5 43.3 %shard_map.113 = (f32[2,2,18,512]{3,2,1,0:T(8,128)}, f32[2,1,4096]{2,1,0:T(1,128)}) custom-call(f32[2,2,18,512]{3,2,1,0:T(8,128)} %bitcast.23, f32[2,18,512]{2,1,0:T(8,128)} %get-tuple-element.13.u_ref, f32[2,18,512]{2,1,0:T(8,128)} %get-tuple-element.12.v_ref, f32[2,2,512]{2,1,0:T(2,128)} %flux.1, bf16[2,96,256]{2,1,0:T(8,128)(2,1)} %bitcast.24, ...), custom_call_target="tpu_custom_call" | custom-call | tf_op jit(solution)/shard_map/pallas_call | solution.py:437
  47.8 0.0 copy-start.4
  47.8 1.7 %copy.23 = f32[2,18,2,512]{3,2,1,0:T(2,128)} copy(f32[2,18,2,512]{3,1,2,0:T(8,128)} %bitcast.25) | data formatting | bytes 294912
  49.5 0.0 copy-done.4
  49.5 0.6 %copy.32 = f32[2,1,4096]{2,0,1:T(2,128)} copy(f32[2,1,4096]{2,1,0:T(1,128)S(1)} %copy-done.4) | data formatting | bytes 65536
  (4 shorter events, 0.1 us)
Async XLA Ops:
  0.6 0.8 %copy-start = (f32[72,72]{1,0:T(8,128)S(1)}, f32[72,72]{1,0:T(8,128)}, u32[]{:S(2)}) copy-start(f32[72,72]{1,0:T(8,128)} %param.14) | copy-start | bytes 62212
  1.9 0.9 %copy-start.1 = (f32[2,18,2,512]{3,2,1,0:T(2,128)S(1)}, f32[2,18,2,512]{3,2,1,0:T(2,128)}, u32[]{:S(2)}) copy-start(f32[2,18,2,512]{3,2,1,0:T(2,128)} %param.10) | copy-start | bytes 442372
  2.8 0.9 %copy-start.2 = (f32[18,2,512]{2,1,0:T(2,128)S(1)}, f32[18,2,512]{2,1,0:T(2,128)}, u32[]{:S(2)}) copy-start(f32[18,2,512]{2,1,0:T(2,128)} %param.12) | copy-start | bytes 221188
  2.8 1.0 %copy-start.3 = (f32[18,2,512]{2,1,0:T(2,128)S(1)}, f32[18,2,512]{2,1,0:T(2,128)}, u32[]{:S(2)}) copy-start(f32[18,2,512]{2,1,0:T(2,128)} %param.11) | copy-start | bytes 221188
  47.8 1.7 %copy-start.4 = (f32[2,1,4096]{2,1,0:T(1,128)S(1)}, f32[2,1,4096]{2,1,0:T(1,128)}, u32[]{:S(2)}) copy-start(f32[2,1,4096]{2,1,0:T(1,128)} %get-tuple-element.5) | copy-start | bytes 98308

commit v5 on v4

--- a/solution.py
+++ b/solution.py
@@ -48,9 +48,9 @@
 
 def kernel_body(
     dims,
-    tracer, u_ref, v_ref, flux, mix, kern, column, owner, offset, counts,
+    tracer, u_in, v_in, flux, mixing, kern, column, owner, offset, counts,
     out, evolved,
-    cur, halo_w, halo_e, halo_u, mixed, mixed_in, rhs, gathered, levs, lhs, onehot, lon_of,
+    mix, u_ref, cur, halo_w, halo_e, halo_u, mixed, mixed_in, rhs, gathered, levs, lhs, onehot, lon_of,
     weight, eff, eff_out, found_at, nums, dens,
     h_send, h_recv, u_sem, z_send, z_recv, w_send, w_recv, g_send, g_recv, n_send, n_recv,
     d_send, d_recv,
@@ -73,8 +73,10 @@
     bottom = jnp.logical_and(row_ids == 0, lev == 0)
     for s in range(scen):
         for i in range(lon_here):
-            here = tracer[s, i]
-            cur[0, s, i] = jnp.where(bottom, here + flux[s, pl.ds(i, 1)], here)
+            here = tracer[s, :, i, :]
+            cur[0, s, i] = jnp.where(bottom, here + flux[s, pl.ds(i, 1), :], here)
+    for i in range(lon_here):
+        u_ref[i] = u_in[:, i, :]
     pl.semaphore_wait(barrier, len(friends))
 
     def remote(src, dst, send, recv, device):
@@ -171,6 +173,38 @@
         onehot[:, at] = (lat_rows == lat).astype(jnp.float32).astype(jnp.bfloat16)
         lon_of[:, at] = owner[:, at] * lon_here + lon_in
         return carry
+
+    def lay_out_mixing():
+        size = nlev * lev_here
+        row = lax.broadcasted_iota(jnp.int32, (4 * PAD, size), 0)
+        col = lax.broadcasted_iota(jnp.int32, (4 * PAD, size), 1)
+        part = sum((row >= PAD * q).astype(jnp.int32) for q in range(1, 4))
+        inner = row - PAD * part
+        second = (part >= 2).astype(jnp.int32)
+        wanted = (half * 2 + second) * lev_here + inner
+        hit = jnp.logical_and(col == wanted, inner < lev_here)
+        is_low = part - 2 * second
+        pick_high = jnp.where(jnp.logical_and(hit, is_low == 0), 1.0, 0.0).astype(jnp.bfloat16)
+        pick_low = jnp.where(jnp.logical_and(hit, is_low == 1), 1.0, 0.0).astype(jnp.bfloat16)
+        at = lax.broadcasted_iota(jnp.int32, (size, nlev * KPAD), 1)
+        here = lax.broadcasted_iota(jnp.int32, (size, nlev * KPAD), 0)
+        block = sum((at >= KPAD * z).astype(jnp.int32) for z in range(1, nlev))
+        inner = at - KPAD * block
+        hit = jnp.logical_and(here == block * lev_here + inner, inner < lev_here)
+        spread = jnp.where(hit, 1.0, 0.0).astype(jnp.bfloat16)
+        high, low = split(mixing[...])
+
+        def dot(a, b, dim):
+            return lax.dot_general(
+                a, b, (((1,), (dim,)), ((), ())), preferred_element_type=jnp.float32
+            )
+
+        for kind in range(2):
+            highs = dot(pick_high, high, kind)
+            both = highs + dot(pick_low, low, kind)
+            for k, rows in enumerate((both, highs)):
+                placed = dot(rows.astype(jnp.bfloat16), spread, 0)
+                mix[kind, :, k * nlev * KPAD:(k + 1) * nlev * KPAD] = placed.astype(jnp.bfloat16)
 
     def mix_blocks(kind, blocks):
         for z, block in enumerate(blocks):
@@ -208,7 +242,7 @@
                 raw_copy(s, k, mate).wait_recv()
             for i in range(lon_here):
                 own, other = mix_blocks(0, [levs[s, z, i] for z in range(nlev)])
-                out[s, i] = own
+                out[s, :, i, :] = own
                 mixed[s, i] = other
             mixed_copy(s).start()
 
@@ -300,6 +334,7 @@
             copy.start()
             num_copies[(s, part)].append(copy)
 
+    lay_out_mixing()
     lax.fori_loop(0, steps // 2, prepare, 0)
     u_copy.wait_recv()
     for step in range(NSUB):
@@ -309,7 +344,7 @@
             cells = [halo_w[step, s]] + [cur[step, s, i] for i in range(lon_here)]
             cells.append(halo_e[step, s])
             winds = [u_ref[i] for i in range(lon_here)] + [halo_u[...]]
-            new = substep(cells, winds, [v_ref[i] for i in range(lon_here)], lat_ids)
+            new = substep(cells, winds, [v_in[:, i, :] for i in range(lon_here)], lat_ids)
             if step < NSUB - 1:
                 for i in range(lon_here):
                     cur[step + 1, s, i] = new[i]
@@ -356,12 +391,12 @@
     wait_weights(3)
     resume(0, groups - 1, steps // 2, steps)
     send_nums(0, 1)
-    mix_levels(0)
     search(1, groups - 1, 0, steps // 2)
     send_nums(1, 0)
-    mix_levels(1)
     resume(1, groups - 1, steps // 2, steps)
     send_nums(1, 1)
+    mix_levels(0)
+    mix_levels(1)
 
     for copy in den_copies:
         copy.wait_recv()
@@ -377,7 +412,7 @@
         num = nums[s, 0]
         for z in range(1, nlev):
             num = num + nums[s, z]
-        evolved[s] = jnp.where(in_use, num / den, 0.0)
+        evolved[pl.ds(s, 1), :] = jnp.where(in_use, num / den, 0.0)
     pending.extend(den_copies)
     for copy in pending:
         copy.wait_send()
@@ -385,7 +420,8 @@
         @pl.when(is_end)
         def _():
             mixed_copy(s).wait_recv()
-            out[s] = mixed_in[s]
+            for i in range(lon_here):
+                out[s, :, i, :] = mixed_in[s, i]
             raw_copy(s, 2, nlev - 1 - mate).wait_send()
             raw_copy(s, 0, mate).wait_send()
 
@@ -411,24 +447,6 @@
     scen, lev_here, lon_here, nlat = tracer.shape
     snd = column.shape[0]
     tiles, nlev = lax.axis_size("tile"), lax.axis_size("lev")
-    lev = lax.axis_index("lev")
-    first = lev // 2 * 2 * lev_here
-    rows = lax.dynamic_slice_in_dim(
-        jnp.stack([mixing, mixing.T]), first, 2 * lev_here, 1
-    )
-    rows = rows.reshape(2, 2, lev_here, nlev, lev_here)
-    rows = jnp.pad(rows, ((0, 0), (0, 0), (0, PAD - lev_here), (0, 0), (0, KPAD - lev_here)))
-    rows = rows.reshape(2, 2, 1, PAD, nlev * KPAD)
-    high = lax.reduce_precision(rows, 8, 7)
-    low = rows - high
-    mix = jnp.concatenate(
-        [
-            jnp.concatenate([high, high], axis=4),
-            jnp.concatenate([low, jnp.zeros_like(low)], axis=4),
-        ],
-        axis=2,
-    )
-    mix = mix.reshape(2, 4 * PAD, 2 * nlev * KPAD).astype(jnp.bfloat16)
     f32, bf16 = jnp.float32, jnp.bfloat16
     block = (lev_here, nlat)
     dma = pltpu.SemaphoreType.DMA
@@ -437,12 +455,14 @@
     out, evolved = pl.pallas_call(
         functools.partial(kernel_body, (scen, lev_here, lon_here, nlat, snd, tiles, nlev)),
         out_shape=(
-            jax.ShapeDtypeStruct((scen, lon_here) + block, f32),
-            jax.ShapeDtypeStruct((scen, 1, snd), f32),
+            jax.ShapeDtypeStruct(tracer.shape, f32),
+            jax.ShapeDtypeStruct((scen, snd), f32),
         ),
         in_specs=[vmem] * 9 + [pl.BlockSpec(memory_space=pltpu.SMEM)],
         out_specs=(vmem, vmem),
         scratch_shapes=[
+            pltpu.VMEM((2, 4 * PAD, 2 * nlev * KPAD), bf16),
+            pltpu.VMEM((lon_here,) + block, f32),
             pltpu.VMEM((NSUB, scen, lon_here) + block, f32),
             pltpu.VMEM((NSUB, scen) + block, f32),
             pltpu.VMEM((NSUB, scen) + block, f32),
@@ -479,18 +499,18 @@
             collective_id=0, has_side_effects=True, vmem_limit_bytes=56 * 2**20
         ),
     )(
-        tracer.transpose(0, 2, 1, 3),
-        u_courant.transpose(1, 0, 2),
-        v_courant.transpose(1, 0, 2),
+        tracer,
+        u_courant,
+        v_courant,
         surface_flux,
-        mix,
+        mixing,
         kernel,
         column[None],
         owner_tile[None],
         offset[None],
         counts,
     )
-    return out.transpose(0, 2, 1, 3), evolved[:, 0]
+    return out, evolved
 
 
 def solution(mesh):

time: 50.4 us -> 46.3 us (0.919)
  local copies, waits for them, and re-layouts: 4.83 us -> 2.2 us
  Pallas kernels: 43.3 us -> 42.6 us
  other arithmetic: 0.67 us -> 0 us
    unnamed x14 -> x4, local copies, waits for them, and re-layouts: 3.77 us -> 2.2 us
    transpose x1 -> x0, local copies, waits for them, and re-layouts: 0.7 us -> none  [body(): v_courant.transpose(1, 0, 2)]
    pallas_call x1, Pallas kernels: 43.3 us -> 42.6 us  [body(): pl.pallas_call(functools.partial(kernel_body, (scen, lev_here, lon_here,...]
    concatenate x1 -> x0, other arithmetic: 0.64 us -> none  [body(): jnp.concatenate([jnp.concatenate([high, high], axis=4), jnp.concatenate([...]
where the time goes in v5:
time: 46.3 us; the launch traced here: 46.1 us
  Pallas kernels  42.6 us (92%)
  local copies, waits for them, and re-layouts  2.2 us (5%)
  between operations  1.3 us (3%)
    pallas_call x1, Pallas kernels, body(): pl.pallas_call(functools.partial(kernel_body, (scen, lev_here, lon_here,...  42.6 us
    unnamed x4, local copies, waits for them, and re-layouts  2.2 us

profile of v5, /device:TPU:0, one launch (start us, length us, event | category | flops | bytes accessed | tf_op | source)
XLA Modules:
  0.0 46.1 jit_solution(10696733998865859592)
XLA Ops:
  1.3 42.6 %shard_map.113 = (f32[2,18,2,512]{3,2,1,0:T(2,128)}, f32[2,4096]{1,0:T(2,128)}) custom-call(f32[2,18,2,512]{3,2,1,0:T(2,128)} %tracer.1, f32[18,2,512]{2,1,0:T(2,128)} %u_in.1, f32[18,2,512]{2,1,0:T(2,128)} %v_in.1, f32[2,2,512]{2,1,0:T(2,128)} %flux.1, f32[72,72]{1,0:T(8,128)} %mixing.1, f32[18,4096]{1,0:T(8,128)} %kern.1, s32[1,4096]{1,0:T(1,128)} %bitcast.3, ...), custom_call_target="tpu_custom_call" | custom-call | tf_op jit(solution)/shard_map/pallas_call | solution.py:455
  43.9 0.0 copy-start
  43.9 1.6 %copy.15 = f32[2,18,2,512]{3,2,1,0:T(2,128)} copy(f32[2,18,2,512]{3,2,1,0:T(2,128)} %get-tuple-element.4) | data formatting | bytes 294912
  45.5 0.0 copy-done
  45.5 0.6 %copy.16 = f32[2,4096]{1,0:T(2,128)} copy(f32[2,4096]{1,0:T(2,128)S(1)} %copy-done) | data formatting | bytes 65536
Async XLA Ops:
  43.9 1.6 %copy-start = (f32[2,4096]{1,0:T(2,128)S(1)}, f32[2,4096]{1,0:T(2,128)}, u32[]{:S(2)}) copy-start(f32[2,4096]{1,0:T(2,128)} %get-tuple-element.5) | copy-start | bytes 98308

commit v6 on v5

--- a/solution.py
+++ b/solution.py
@@ -283,45 +283,55 @@
         blocks = [grow(gathered[s, m, i], PAD) for i in range(lon_here)]
         high, low = split(jnp.concatenate(blocks, axis=0))
         place = arrivals(s).index(m)
-        at = place % GROUP * lon_here * PAD
-        lhs[s, place // GROUP, at:at + lon_here * PAD, 0:nlat] = high
-        lhs[s, place // GROUP, at:at + lon_here * PAD, nlat:2 * nlat] = low
+        at = (s * GROUP + place % GROUP) * lon_here * PAD
+        lhs[place // GROUP, at:at + lon_here * PAD, 0:nlat] = high
+        lhs[place // GROUP, at:at + lon_here * PAD, nlat:2 * nlat] = low
 
     groups = tiles // GROUP
 
     num_copies = {}
 
-    def search(s, group, low, high):
-        slots = arrivals(s)[group * GROUP:(group + 1) * GROUP]
-        for m in slots:
-            if m % 2 == 1:
-                block_copy(s, m - 1, 1).wait_recv()
-                load_columns(s, m)
-        resume(s, group, low, high)
-
-    def resume(s, group, low, high):
-        slots = arrivals(s)[group * GROUP:(group + 1) * GROUP]
+    def complete(group):
+        for s in range(scen):
+            for m in arrivals(s)[group * GROUP:(group + 1) * GROUP]:
+                if m % 2 == 1:
+                    block_copy(s, m - 1, 1).wait_recv()
+                    load_columns(s, m)
+
+    def search(group, part):
+        pieces = range(0, PAD, 8)
 
         def one_step(nb, carry):
             at = pl.ds(pl.multiple_of(nb * NB, NB), NB)
             hot = onehot[:, at]
             twice = jnp.concatenate([hot, hot], axis=0)
-            lon_ids = jnp.broadcast_to(lon_of[:, at], (PAD, NB))
-            found = jnp.dot(lhs[s, group], twice, preferred_element_type=jnp.float32)
-            acc = jnp.zeros((PAD, NB), jnp.float32) if group == 0 else found_at[s, :, at]
-            for inner, m in enumerate(slots):
-                tile = jnp.bitwise_xor(me, m)
-                for i in range(lon_here):
-                    r = (inner * lon_here + i) * PAD
-                    acc = jnp.where(lon_ids == tile * lon_here + i, found[r:r + PAD], acc)
-            if group < groups - 1:
-                found_at[s, :, at] = acc
-            else:
-                terms = acc[0:lev_here] * eff[:, at]
-                nums[s, lev, :, at] = jnp.sum(terms, axis=0, keepdims=True)
+            lon_ids = jnp.broadcast_to(lon_of[:, at], (8, NB))
+            found = jnp.dot(lhs[group], twice, preferred_element_type=jnp.float32)
+            for s in range(scen):
+                if group == 0:
+                    acc = [jnp.zeros((8, NB), jnp.float32) for _ in pieces]
+                else:
+                    acc = [found_at[s, q:q + 8, at] for q in pieces]
+                slots = arrivals(s)[group * GROUP:(group + 1) * GROUP]
+                for inner, m in enumerate(slots):
+                    tile = jnp.bitwise_xor(me, m)
+                    for i in range(lon_here):
+                        r = ((s * GROUP + inner) * lon_here + i) * PAD
+                        here = lon_ids == tile * lon_here + i
+                        acc = [
+                            jnp.where(here, found[r + q:r + q + 8], old)
+                            for q, old in zip(pieces, acc)
+                        ]
+                if group < groups - 1:
+                    for q, value in zip(pieces, acc):
+                        found_at[s, q:q + 8, at] = value
+                else:
+                    whole = jnp.concatenate(acc, axis=0)
+                    terms = whole[0:lev_here] * eff[:, at]
+                    nums[s, lev, :, at] = jnp.sum(terms, axis=0, keepdims=True)
             return carry
 
-        lax.fori_loop(low, high, one_step, 0, unroll=2)
+        lax.fori_loop(part * steps // 2, (part + 1) * steps // 2, one_step, 0, unroll=2)
 
     def send_nums(s, part):
         at = pl.ds(part * (snd // 2), snd // 2)
@@ -370,30 +380,31 @@
     mix_weights(0)
     forward(0, 1)
     forward(1, 1)
-    search(0, 0, 0, steps)
+    complete(0)
+    search(0, 0)
     forward(0, 2)
+    forward(1, 2)
     mix_weights(1)
-    search(1, 0, 0, steps)
-    forward(1, 2)
+    search(0, 1)
     for p in range(3, hops + 1):
         forward(0, p)
         forward(1, p)
     mix_weights(2)
     for group in range(1, groups - 1):
-        search(0, group, 0, steps)
-        search(1, group, 0, steps)
+        complete(group)
+        search(group, 0)
+        search(group, 1)
     mix_weights(3)
+    complete(groups - 1)
     wait_weights(0)
     wait_weights(1)
-    search(0, groups - 1, 0, steps // 2)
+    search(groups - 1, 0)
     send_nums(0, 0)
+    send_nums(1, 0)
     wait_weights(2)
     wait_weights(3)
-    resume(0, groups - 1, steps // 2, steps)
+    search(groups - 1, 1)
     send_nums(0, 1)
-    search(1, groups - 1, 0, steps // 2)
-    send_nums(1, 0)
-    resume(1, groups - 1, steps // 2, steps)
     send_nums(1, 1)
     mix_levels(0)
     mix_levels(1)
@@ -472,7 +483,7 @@
             pltpu.VMEM((2 * nlev * KPAD, nlat), bf16),
             pltpu.VMEM((scen, tiles, lon_here) + block, f32),
             pltpu.VMEM((scen, nlev, lon_here) + block, f32),
-            pltpu.VMEM((scen, groups, GROUP * lon_here * PAD, 2 * nlat), bf16),
+            pltpu.VMEM((groups, scen * GROUP * lon_here * PAD, 2 * nlat), bf16),
             pltpu.VMEM((nlat, snd), bf16),
             pltpu.VMEM((1, snd), jnp.int32),
             pltpu.VMEM((nlev, lev_here, snd), f32),

time: 46.3 us -> 44.8 us (0.968)
  Pallas kernels: 42.6 us -> 41.1 us
    pallas_call x1, Pallas kernels: 42.6 us -> 41.1 us  [body(): pl.pallas_call(functools.partial(kernel_body, (scen, lev_here, lon_here,...]
where the time goes in v6:
time: 44.8 us; the launch traced here: 44.6 us
  Pallas kernels  41.1 us (92%)
  local copies, waits for them, and re-layouts  2.2 us (5%)
  between operations  1.3 us (3%)
    pallas_call x1, Pallas kernels, body(): pl.pallas_call(functools.partial(kernel_body, (scen, lev_here, lon_here,...  41.1 us
    unnamed x4, local copies, waits for them, and re-layouts  2.2 us

profile of v6, /device:TPU:0, one launch (start us, length us, event | category | flops | bytes accessed | tf_op | source)
XLA Modules:
  0.0 44.6 jit_solution(9900881051355841110)
XLA Ops:
  1.3 41.1 %shard_map.113 = (f32[2,18,2,512]{3,2,1,0:T(2,128)}, f32[2,4096]{1,0:T(2,128)}) custom-call(f32[2,18,2,512]{3,2,1,0:T(2,128)} %tracer.1, f32[18,2,512]{2,1,0:T(2,128)} %u_in.1, f32[18,2,512]{2,1,0:T(2,128)} %v_in.1, f32[2,2,512]{2,1,0:T(2,128)} %flux.1, f32[72,72]{1,0:T(8,128)} %mixing.1, f32[18,4096]{1,0:T(8,128)} %kern.1, s32[1,4096]{1,0:T(1,128)} %bitcast.3, ...), custom_call_target="tpu_custom_call" | custom-call | tf_op jit(solution)/shard_map/pallas_call | solution.py:466
  42.4 0.0 copy-start
  42.4 1.6 %copy.15 = f32[2,18,2,512]{3,2,1,0:T(2,128)} copy(f32[2,18,2,512]{3,2,1,0:T(2,128)} %get-tuple-element.4) | data formatting | bytes 294912
  44.0 0.0 copy-done
  44.0 0.6 %copy.16 = f32[2,4096]{1,0:T(2,128)} copy(f32[2,4096]{1,0:T(2,128)S(1)} %copy-done) | data formatting | bytes 65536
Async XLA Ops:
  42.4 1.6 %copy-start = (f32[2,4096]{1,0:T(2,128)S(1)}, f32[2,4096]{1,0:T(2,128)}, u32[]{:S(2)}) copy-start(f32[2,4096]{1,0:T(2,128)} %get-tuple-element.5) | copy-start | bytes 98308

commit v7 on v6

--- a/solution.py
+++ b/solution.py
@@ -401,13 +401,13 @@
     search(groups - 1, 0)
     send_nums(0, 0)
     send_nums(1, 0)
+    mix_levels(0)
+    mix_levels(1)
     wait_weights(2)
     wait_weights(3)
     search(groups - 1, 1)
     send_nums(0, 1)
     send_nums(1, 1)
-    mix_levels(0)
-    mix_levels(1)
 
     for copy in den_copies:
         copy.wait_recv()

time: 44.8 us -> 46.5 us (1.038)
  Pallas kernels: 41.1 us -> 42.8 us
    pallas_call x1, Pallas kernels: 41.1 us -> 42.8 us  [body(): pl.pallas_call(functools.partial(kernel_body, (scen, lev_here, lon_here,...]
where the time goes in v7:
time: 46.5 us; the launch traced here: 46.3 us
  Pallas kernels  42.8 us (92%)
  local copies, waits for them, and re-layouts  2.2 us (5%)
  between operations  1.3 us (3%)
    pallas_call x1, Pallas kernels, body(): pl.pallas_call(functools.partial(kernel_body, (scen, lev_here, lon_here,...  42.8 us
    unnamed x4, local copies, waits for them, and re-layouts  2.2 us

profile of v7, /device:TPU:0, one launch (start us, length us, event | category | flops | bytes accessed | tf_op | source)
XLA Modules:
  0.0 46.3 jit_solution(4507196904353186324)
XLA Ops:
  1.3 42.8 %shard_map.113 = (f32[2,18,2,512]{3,2,1,0:T(2,128)}, f32[2,4096]{1,0:T(2,128)}) custom-call(f32[2,18,2,512]{3,2,1,0:T(2,128)} %tracer.1, f32[18,2,512]{2,1,0:T(2,128)} %u_in.1, f32[18,2,512]{2,1,0:T(2,128)} %v_in.1, f32[2,2,512]{2,1,0:T(2,128)} %flux.1, f32[72,72]{1,0:T(8,128)} %mixing.1, f32[18,4096]{1,0:T(8,128)} %kern.1, s32[1,4096]{1,0:T(1,128)} %bitcast.3, ...), custom_call_target="tpu_custom_call" | custom-call | tf_op jit(solution)/shard_map/pallas_call | solution.py:466
  44.1 0.0 copy-start
  44.1 1.6 %copy.15 = f32[2,18,2,512]{3,2,1,0:T(2,128)} copy(f32[2,18,2,512]{3,2,1,0:T(2,128)} %get-tuple-element.4) | data formatting | bytes 294912
  45.7 0.0 copy-done
  45.7 0.6 %copy.16 = f32[2,4096]{1,0:T(2,128)} copy(f32[2,4096]{1,0:T(2,128)S(1)} %copy-done) | data formatting | bytes 65536
Async XLA Ops:
  44.1 1.6 %copy-start = (f32[2,4096]{1,0:T(2,128)S(1)}, f32[2,4096]{1,0:T(2,128)}, u32[]{:S(2)}) copy-start(f32[2,4096]{1,0:T(2,128)} %get-tuple-element.5) | copy-start | bytes 98308

commit v8 on v6

--- a/solution.py
+++ b/solution.py
@@ -322,13 +322,18 @@
                             jnp.where(here, found[r + q:r + q + 8], old)
                             for q, old in zip(pieces, acc)
                         ]
-                if group < groups - 1:
-                    for q, value in zip(pieces, acc):
-                        found_at[s, q:q + 8, at] = value
-                else:
-                    whole = jnp.concatenate(acc, axis=0)
-                    terms = whole[0:lev_here] * eff[:, at]
-                    nums[s, lev, :, at] = jnp.sum(terms, axis=0, keepdims=True)
+                for q, value in zip(pieces, acc):
+                    found_at[s, q:q + 8, at] = value
+            return carry
+
+        lax.fori_loop(part * steps // 2, (part + 1) * steps // 2, one_step, 0, unroll=2)
+
+    def finish(part):
+        def one_step(nb, carry):
+            at = pl.ds(pl.multiple_of(nb * NB, NB), NB)
+            for s in range(scen):
+                terms = found_at[s, 0:lev_here, at] * eff[:, at]
+                nums[s, lev, :, at] = jnp.sum(terms, axis=0, keepdims=True)
             return carry
 
         lax.fori_loop(part * steps // 2, (part + 1) * steps // 2, one_step, 0, unroll=2)
@@ -389,23 +394,21 @@
     for p in range(3, hops + 1):
         forward(0, p)
         forward(1, p)
-    mix_weights(2)
     for group in range(1, groups - 1):
         complete(group)
         search(group, 0)
         search(group, 1)
+    complete(groups - 1)
+    search(groups - 1, 0)
+    mix_weights(2)
     mix_weights(3)
-    complete(groups - 1)
-    wait_weights(0)
-    wait_weights(1)
-    search(groups - 1, 0)
-    send_nums(0, 0)
-    send_nums(1, 0)
-    wait_weights(2)
-    wait_weights(3)
     search(groups - 1, 1)
-    send_nums(0, 1)
-    send_nums(1, 1)
+    for part in range(2):
+        for c in range(part * CHUNKS // 2, (part + 1) * CHUNKS // 2):
+            wait_weights(c)
+        finish(part)
+        for s in range(scen):
+            send_nums(s, part)
     mix_levels(0)
     mix_levels(1)
 

time: 44.8 us -> 45.5 us (1.016)
  Pallas kernels: 41.1 us -> 41.8 us
    pallas_call x1, Pallas kernels: 41.1 us -> 41.8 us  [body(): pl.pallas_call(functools.partial(kernel_body, (scen, lev_here, lon_here,...]
where the time goes in v8:
time: 45.5 us; the launch traced here: 45.3 us
  Pallas kernels  41.8 us (92%)
  local copies, waits for them, and re-layouts  2.2 us (5%)
  between operations  1.3 us (3%)
    pallas_call x1, Pallas kernels, body(): pl.pallas_call(functools.partial(kernel_body, (scen, lev_here, lon_here,...  41.8 us
    unnamed x4, local copies, waits for them, and re-layouts  2.2 us

profile of v8, /device:TPU:0, one launch (start us, length us, event | category | flops | bytes accessed | tf_op | source)
XLA Modules:
  0.0 45.3 jit_solution(3632662818815870985)
XLA Ops:
  1.3 41.8 %shard_map.113 = (f32[2,18,2,512]{3,2,1,0:T(2,128)}, f32[2,4096]{1,0:T(2,128)}) custom-call(f32[2,18,2,512]{3,2,1,0:T(2,128)} %tracer.1, f32[18,2,512]{2,1,0:T(2,128)} %u_in.1, f32[18,2,512]{2,1,0:T(2,128)} %v_in.1, f32[2,2,512]{2,1,0:T(2,128)} %flux.1, f32[72,72]{1,0:T(8,128)} %mixing.1, f32[18,4096]{1,0:T(8,128)} %kern.1, s32[1,4096]{1,0:T(1,128)} %bitcast.3, ...), custom_call_target="tpu_custom_call" | custom-call | tf_op jit(solution)/shard_map/pallas_call | solution.py:469
  43.1 0.0 copy-start
  43.1 1.6 %copy.15 = f32[2,18,2,512]{3,2,1,0:T(2,128)} copy(f32[2,18,2,512]{3,2,1,0:T(2,128)} %get-tuple-element.4) | data formatting | bytes 294912
  44.7 0.0 copy-done
  44.7 0.6 %copy.16 = f32[2,4096]{1,0:T(2,128)} copy(f32[2,4096]{1,0:T(2,128)S(1)} %copy-done) | data formatting | bytes 65536
Async XLA Ops:
  43.1 1.6 %copy-start = (f32[2,4096]{1,0:T(2,128)S(1)}, f32[2,4096]{1,0:T(2,128)}, u32[]{:S(2)}) copy-start(f32[2,4096]{1,0:T(2,128)} %get-tuple-element.5) | copy-start | bytes 98308
